TPU v7x, 128 devices: a whole 4x4x4 slice. The times are simulated.
128 devices in a mesh: leaf: 16 (over x, y), sub: 8 (over z, core).
Axes of the slice: x: 4, y: 4, z: 4, core: 2. Of those that a mesh axis runs over, the one named last changes fastest.
Arguments:
- charges: bfloat16 [32, 2097152], P(None, ('leaf', 'sub')), may hold values from -0.59765625 to 0.59765625
- points: float32 [3, 2097152], P(None, ('leaf', 'sub')), as said below
- basis: bfloat16 [16384, 64, 128], P(('leaf', 'sub')), may hold values from -0.5 to 0.5
- transfer: float32 [2, 64, 64], replicated, may hold values from -0.625 to 0.625
- near_list: int32 [16384, 8], P(('leaf', 'sub')), may hold values from -1 to 16383, as said below
- coupling_list: int32 [16384, 8], P(('leaf', 'sub')), may hold values from -1 to 16383, as said below
Outputs:
- potential: float32 [32, 2097152], P(None, ('leaf', 'sub'))
Inputs may be any that keep to these rules, and one draw needn't show every extreme that they name: `near_list`: every live slot of row i holds a leaf j with |j - i| <= 64 whose unit box touches the box of leaf i (the box corners differ by at most 1 in every coordinate); slot 0 holds i itself, slot 1 the leaf whose index differs from i in the lowest bit, slot 2 the leaf i - 4 (i + 4 where i < 4), slot 3 the leaf i + 4 (i - 4 where i + 4 >= 16384); other slots may repeat leaves; empty slots hold -1 and come after the live ones; at least four slots of every row are live, and how many are live varies from device to device. `coupling_list`: every live slot of row i holds a leaf j with 1 <= |j - i| <= 64 whose unit box does not touch the box of leaf i (the box corners differ by 2 or more in some coordinate); slot 1 holds a leaf exactly 64 away from i; other slots may repeat leaves; empty slots hold -1 and come after the live ones; at least two slots of every row are live, and how many are live varies from device to device. The points of leaf c lie in the unit box whose lower corner is (c % 2, (c // 2) % 2, c // 4).
All inputs are finite; a program needn't handle non-finite values.
Results may differ from a plain program's by a relative error of at most 0.00065.
The roundings to bfloat16 on the way count: a program that leaves them out, or rounds other values in their place, can miss the bound.
Values may be sent and summed in bfloat16 or wider, within the bound.
A program may use at most 128 MiB of HBM per device.

v0:
```python
import math

import jax
import jax.numpy as jnp
from jax import lax
from jax.sharding import PartitionSpec as P

P_SIZE = 128
K = 64
R = 32
LD = 128


LENGTH_SCALE = 2.0
NUGGET_VARIANCE = 1.0
HIGHEST = lax.Precision.HIGHEST


def padded(block, sides, width):
    for axis, dim in sides:
        count = lax.axis_size(axis)
        forward = [(i, i + 1) for i in range(count - 1)]
        backward = [(target, source) for source, target in forward]
        low = lax.ppermute(
            lax.slice_in_dim(block, block.shape[dim] - width, None, axis=dim), axis, forward
        )
        high = lax.ppermute(lax.slice_in_dim(block, 0, width, axis=dim), axis, backward)
        block = jnp.concatenate([low, block, high], axis=dim)
    return block


def partner(value, axis, stride):
    mask = 2**stride
    pairs = [(source, source ^ mask) for source in range(lax.axis_size(axis))]
    return lax.ppermute(value, axis, pairs)


def unit_nodes():
    index_row = jnp.arange(64, dtype=jnp.int32)

    def axis_value(digit):
        return jnp.cos((2.0 * digit.astype(jnp.float32) + 1.0) * (math.pi / 8.0))

    return jnp.stack(
        [axis_value(index_row // 16), axis_value(index_row // 4 % 4), axis_value(index_row % 4)]
    )


def covariance(first, second):
    separation = first[..., :, None] - second[..., None, :]
    return jnp.exp(-jnp.sqrt(jnp.sum(separation * separation, axis=0)) / LENGTH_SCALE)


def cluster_nodes(centers, radii, reference_nodes):
    extra = (1,) * (centers.ndim - 1)
    shaped = reference_nodes.reshape((3,) + extra + (reference_nodes.shape[1],))
    return centers[..., None] + radii[None, ..., None] * shaped


def leaf_shapes(leaf_points):
    centers = jnp.mean(leaf_points, axis=2)
    offsets = leaf_points - centers[:, :, None]
    radii = jnp.max(jnp.sqrt(jnp.sum(offsets * offsets, axis=0)), axis=1)
    return (centers, radii)


def merge_shapes(centers, radii):
    paired = centers.reshape(3, -1, 2)
    spread = radii.reshape(-1, 2)
    separation = paired[:, :, 0] - paired[:, :, 1]
    joined = 0.5 * (paired[:, :, 0] + paired[:, :, 1])
    return (
        joined,
        jnp.maximum(spread[:, 0], spread[:, 1])
        + 0.5 * jnp.sqrt(jnp.sum(separation * separation, axis=0)),
    )


def merge_coefficients(coefficient, transfer):
    paired = coefficient.reshape(coefficient.shape[0], -1, 2, coefficient.shape[2])
    return jnp.einsum("rcsk,skj->rcj", paired, transfer, precision=HIGHEST)


def descend(downward, transfer):
    spread = jnp.einsum("rcj,skj->rcsk", downward, transfer, precision=HIGHEST)
    return spread.reshape(downward.shape[0], -1, downward.shape[2])


def sibling_coupling(coefficient, centers, radii, reference_nodes):
    nodes = cluster_nodes(centers, radii, reference_nodes)
    paired = nodes.reshape(3, -1, 2, nodes.shape[2])
    kernel_tile = covariance(paired[:, :, 0], paired[:, :, 1])
    coef_pairs = coefficient.reshape(coefficient.shape[0], -1, 2, coefficient.shape[2])
    to_left = jnp.einsum("rcq,cpq->rcp", coef_pairs[:, :, 1], kernel_tile, precision=HIGHEST)
    to_right = jnp.einsum("rcp,cpq->rcq", coef_pairs[:, :, 0], kernel_tile, precision=HIGHEST)
    return jnp.stack([to_left, to_right], axis=2).reshape(coefficient.shape)


def listed_coupling(
    all_coef, all_centers, all_radii, own_centers, own_radii, slot_rows, reference_nodes
):
    is_live = slot_rows >= 0
    safe_rows = jnp.where(is_live, slot_rows, 0)
    own_nodes = cluster_nodes(own_centers, own_radii, reference_nodes)
    far_nodes = cluster_nodes(
        jnp.take(all_centers, safe_rows, axis=1),
        jnp.take(all_radii, safe_rows, axis=0),
        reference_nodes,
    )
    kernel_tile = (
        covariance(own_nodes[:, :, None, :], far_nodes)
        * is_live.astype(jnp.float32)[:, :, None, None]
    )
    far_coef = jnp.take(all_coef, safe_rows, axis=1)
    return jnp.einsum("wspq,rwsq->rwp", kernel_tile, far_coef, precision=HIGHEST)


def near_tile(all_x, all_points, own_x, own_points, slot_rows):
    is_live = slot_rows >= 0
    safe_rows = jnp.where(is_live, slot_rows, 0)
    far_points = jnp.take(all_points, safe_rows, axis=1)
    kernel_tile = (
        covariance(own_points[:, :, None, :], far_points)
        * is_live.astype(jnp.float32)[:, :, None, None]
    ).astype(jnp.bfloat16)
    far_x = jnp.take(all_x, safe_rows, axis=1)
    summed = jnp.einsum("wspq,rwsq->rwp", kernel_tile, far_x, preferred_element_type=jnp.float32)
    return summed + NUGGET_VARIANCE * own_x.astype(jnp.float32)


def blocked(function, total_rows, block_size):
    starts = jnp.arange(total_rows // block_size, dtype=jnp.int32) * block_size
    pieces = lax.map(function, starts)
    return jnp.moveaxis(pieces, 0, 1).reshape(pieces.shape[1], total_rows, pieces.shape[3])


def pick_column(values, position):
    columns = jnp.arange(values.shape[-1], dtype=jnp.int32)
    return jnp.sum(jnp.where(columns == position, values, 0.0), axis=-1)


def per_device(charges, points, basis, transfer, near_list, coupling_list):
    reference_nodes = unit_nodes()
    device = lax.axis_index(("leaf", "sub"))
    devices_count = lax.axis_size(("leaf", "sub"))
    tree_depth = devices_count.bit_length() - 1
    margin = LD
    wide_x = padded(charges, ((("leaf", "sub"), 1),), margin * P_SIZE)
    wide_points = padded(points, ((("leaf", "sub"), 1),), margin * P_SIZE)
    leaf_x = charges.reshape(R, LD, P_SIZE)
    leaf_points = points.reshape(3, LD, P_SIZE)
    ext_x = wide_x.reshape(R, LD + 2 * margin, P_SIZE)
    ext_points = wide_points.reshape(3, LD + 2 * margin, P_SIZE)
    first_leaf = device * LD - margin
    local_near = jnp.where(near_list >= 0, near_list - first_leaf, -1)
    local_coupling = jnp.where(coupling_list >= 0, coupling_list - first_leaf, -1)
    block_size = min(16, LD)

    def near_block(start_leaf):
        return near_tile(
            ext_x,
            ext_points,
            lax.dynamic_slice_in_dim(leaf_x, start_leaf, block_size, 1),
            lax.dynamic_slice_in_dim(leaf_points, start_leaf, block_size, 1),
            lax.dynamic_slice_in_dim(local_near, start_leaf, block_size, 0),
        )

    near = blocked(near_block, LD, block_size)
    coefficient = jnp.einsum("rcp,ckp->rck", leaf_x, basis, preferred_element_type=jnp.float32)
    centers, radii = leaf_shapes(leaf_points)
    wide_coef = padded(coefficient, ((("leaf", "sub"), 1),), margin)
    ext_centers, ext_radii = leaf_shapes(ext_points)

    def couple_block(start_leaf):
        return listed_coupling(
            wide_coef,
            ext_centers,
            ext_radii,
            lax.dynamic_slice_in_dim(centers, start_leaf, block_size, 1),
            lax.dynamic_slice_in_dim(radii, start_leaf, block_size, 0),
            lax.dynamic_slice_in_dim(local_coupling, start_leaf, block_size, 0),
            reference_nodes,
        )

    leaf_couple = blocked(couple_block, LD, block_size)
    levels = [(coefficient, centers, radii)]
    while levels[-1][0].shape[1] > 1:
        last_coef, last_centers, last_radii = levels[-1]
        joined_centers, joined_radii = merge_shapes(last_centers, last_radii)
        levels.append((merge_coefficients(last_coef, transfer), joined_centers, joined_radii))
    root_coef = levels[-1][0][:, 0, :]
    root_centers, root_radii = (
        lax.all_gather(levels[-1][1], ("leaf", "sub"), axis=1, tiled=True),
        lax.all_gather(levels[-1][2], ("leaf", "sub"), axis=0, tiled=True),
    )
    top_shapes = [(root_centers, root_radii)]
    for level_index in range(tree_depth - 1):
        top_shapes.append(merge_shapes(top_shapes[-1][0], top_shapes[-1][1]))
    own_coef = root_coef
    couplings = []
    side_bits = []
    for level_index in range(tree_depth):
        sibling_coef = partner(own_coef, ("leaf", "sub"), level_index)
        node_index = jnp.right_shift(device, level_index)
        side_bit = node_index % 2
        level_centers, level_radii = top_shapes[level_index]
        own_nodes = cluster_nodes(
            pick_column(level_centers, node_index),
            pick_column(level_radii, node_index),
            reference_nodes,
        )
        far_nodes = cluster_nodes(
            pick_column(level_centers, node_index ^ 1),
            pick_column(level_radii, node_index ^ 1),
            reference_nodes,
        )
        kernel_tile = covariance(own_nodes, far_nodes)
        couplings.append(jnp.einsum("rq,pq->rp", sibling_coef, kernel_tile, precision=HIGHEST))
        side_bits.append(side_bit)
        if level_index + 1 < tree_depth:
            is_left = side_bit == 0
            left_coef = jnp.where(is_left, own_coef, sibling_coef)
            right_coef = jnp.where(is_left, sibling_coef, own_coef)
            own_coef = jnp.einsum(
                "rsk,skj->rj",
                jnp.stack([left_coef, right_coef], axis=1),
                transfer,
                precision=HIGHEST,
            )
    root_down = jnp.zeros((R, K), jnp.float32)
    for level_index in reversed(range(tree_depth)):
        chosen = jnp.where(side_bits[level_index] == 0, transfer[0], transfer[1])
        root_down = couplings[level_index] + jnp.einsum(
            "rj,kj->rk", root_down, chosen, precision=HIGHEST
        )
    downward = root_down[:, None, :]
    for level_index in range(len(levels) - 2, 0, -1):
        level_coef, level_centers, level_radii = levels[level_index]
        downward = descend(downward, transfer) + sibling_coupling(
            level_coef, level_centers, level_radii, reference_nodes
        )
    downward = descend(downward, transfer) + leaf_couple
    far = jnp.einsum(
        "rck,ckp->rcp", downward.astype(jnp.bfloat16), basis, preferred_element_type=jnp.float32
    )
    return (near + far).reshape(R, LD * P_SIZE)


def solution(mesh):
    in_specs = (
        P(None, ("leaf", "sub")),
        P(None, ("leaf", "sub")),
        P(("leaf", "sub"), None, None),
        P(),
        P(("leaf", "sub"), None),
        P(("leaf", "sub"), None),
    )
    out_specs = P(None, ("leaf", "sub"))
    return jax.shard_map(
        per_device, mesh=mesh, in_specs=in_specs, out_specs=out_specs, check_vma=False
    )
```

profile of v0, /device:TPU:4, one launch (start us, length us, event | category | flops | bytes accessed | tf_op | source)
XLA Modules:
  0.0 669.6 jit_solution(8263946799317832108)
XLA Ops:
  2.1 7.9 %collective-permute-start.3 = (f32[3,16384]{1,0:T(4,128)}, f32[3,16384]{1,0:T(4,128)}, u32[]{:S(2)}, u32[]{:S(2)}) collective-permute-start(f32[3,16384]{1,0:T(4,128)} %param.11), channel_id=1, source_target_pairs={{1,0},{2,1},{3,2},{4,3},{5,4},{6,5},{7,6},{8,7},{9,8},{10,9},{11,1... | collective-permute-start | bytes 589832 | tf_op jit(solution)/shard_map/ppermute | solution.py:27
  9.9 3.8 fusion.231
  13.7 3.6 copy.231
  19.3 7.9 %collective-permute-start.12 = (f32[32,128,64]{1,2,0:T(8,128)}, f32[32,128,64]{1,2,0:T(8,128)}, u32[]{:S(2)}, u32[]{:S(2)}) collective-permute-start(f32[32,128,64]{1,2,0:T(8,128)} %copy.231), channel_id=1, source_target_pairs={{1,0},{2,1},{3,2},{4,3},{5,4},{6,5},{7,6},{8,7},{9,8},{10,9},{11,1... | collective-permute-start | bytes 3145736 | tf_op jit(solution)/shard_map/ppermute | solution.py:27
  27.2 4.6 fusion.40
  50.7 64.0 %all-reduce = f32[128]{0:T(128)} all-reduce(f32[128]{0:T(128)S(1)} %fusion.203), channel_id=1, replica_groups=mesh['leaf'=16,'sub'=8] {'leaf','sub'}, use_global_device_ids=true, to_apply=%add | all-reduce | flops 128 | bytes 1024
  120.6 29.1 %all-gather = f32[3,128,1]{0,2,1:T(1,128)S(1)} all-gather(f32[3,1,1]{0,2,1:T(1,128)} %get-tuple-element.301), channel_id=2, replica_groups=mesh['leaf'=16,'sub'=8] {'leaf','sub'}, dimensions={1}, use_global_device_ids=true | all-gather | bytes 1548 | tf_op jit(solution)/shard_map/all_gather | solution.py:193
  157.9 3.2 multiply_add_fusion.21
  196.8 3.1 fusion.46
  199.9 3.5 fusion.45
  217.1 3.3 multiply_add_fusion.15
  220.4 3.2 multiply_add_fusion.12
  227.2 2.7 collective-permute-done.5
  239.9 2.7 collective-permute-done.7
  252.1 3.3 collective-permute-done.9
  278.9 3.1 fusion.63
  282.0 7.8 %collective-permute-start.1 = (bf16[32,16384]{1,0:T(8,128)(2,1)S(1)}, bf16[32,16384]{1,0:T(8,128)(2,1)}, u32[]{:S(2)}, u32[]{:S(2)}) collective-permute-start(bf16[32,16384]{1,0:T(8,128)(2,1)S(1)} %copy-done.2), channel_id=1, source_target_pairs={{1,0},{2,1},{3,2},{4,3},{5,4},{6,5},{7,6},{8,7},{9,8},{10,9},{11,1... | collective-permute-start | bytes 3145736 | tf_op jit(solution)/shard_map/ppermute | solution.py:27
  297.3 4.1 copy.233
  301.4 4.0 copy.234
  305.4 6.3 pad_maximum_fusion
  311.7 182.6 %while.21 = (s32[]{:T(128)}, f32[8,32,16,64]{3,1,2,0:T(8,128)}, s32[8]{0:T(128)S(1)}, s32[128,8]{0,1:T(8,128)S(1)}, f32[32,384,64]{2,0,1:T(8,128)}, /*index=5*/f...) while((s32[]{:T(128)}, f32[8,32,16,64]{3,1,2,0:T(8,128)}, ...), condition=%wide.region_65.66_spmd, body=%wide.region_63.65_spmd.sunk | while | flops 207414656 | bytes 10999095 | solution.py:133
  317.4 3.7 multiply_reduce_fusion.37
  321.1 4.8 gather_fusion.4
  325.9 8.9 %fusion.286 = f32[8,32,16,64]{3,1,2,0:T(8,128)} fusion(f32[8,32,16,64]{3,1,2,0:T(8,128)} %get-tuple-element.458, s32[]{:T(128)} %get-tuple-element.457, f32[16,8,64,64]{3,2,1,0:T(8,128)} %multiply_reduce_fusion.37, f32[16,8]{1,0:T(8,128)S(1)} %compare_convert_fusion.5, f32[16,8,32,64]{3,2,1,0:T(8,128)} %bitcast.468, ...), kind=kOutput, calls=%fused_computation.38.clone.1 | convolution fusion | flops 203161600 | bytes 6554752 | tf_op jit(solution)/shard_map/while/body/eval_jaxpr/wspq,rwsq->rwp/dot_general | solution.py:115
  340.2 3.7 multiply_reduce_fusion.37
  343.9 4.8 gather_fusion.4
  348.7 8.9 %fusion.286 = f32[8,32,16,64]{3,1,2,0:T(8,128)} fusion(f32[8,32,16,64]{3,1,2,0:T(8,128)} %get-tuple-element.458, s32[]{:T(128)} %get-tuple-element.457, f32[16,8,64,64]{3,2,1,0:T(8,128)} %multiply_reduce_fusion.37, f32[16,8]{1,0:T(8,128)S(1)} %compare_convert_fusion.5, f32[16,8,32,64]{3,2,1,0:T(8,128)} %bitcast.468, ...), kind=kOutput, calls=%fused_computation.38.clone.1 | convolution fusion | flops 203161600 | bytes 6554752 | tf_op jit(solution)/shard_map/while/body/eval_jaxpr/wspq,rwsq->rwp/dot_general | solution.py:115
  363.0 3.7 multiply_reduce_fusion.37
  366.7 4.8 gather_fusion.4
  371.5 8.9 %fusion.286 = f32[8,32,16,64]{3,1,2,0:T(8,128)} fusion(f32[8,32,16,64]{3,1,2,0:T(8,128)} %get-tuple-element.458, s32[]{:T(128)} %get-tuple-element.457, f32[16,8,64,64]{3,2,1,0:T(8,128)} %multiply_reduce_fusion.37, f32[16,8]{1,0:T(8,128)S(1)} %compare_convert_fusion.5, f32[16,8,32,64]{3,2,1,0:T(8,128)} %bitcast.468, ...), kind=kOutput, calls=%fused_computation.38.clone.1 | convolution fusion | flops 203161600 | bytes 6554752 | tf_op jit(solution)/shard_map/while/body/eval_jaxpr/wspq,rwsq->rwp/dot_general | solution.py:115
  385.8 3.7 multiply_reduce_fusion.37
  389.5 4.8 gather_fusion.4
  394.2 8.9 %fusion.286 = f32[8,32,16,64]{3,1,2,0:T(8,128)} fusion(f32[8,32,16,64]{3,1,2,0:T(8,128)} %get-tuple-element.458, s32[]{:T(128)} %get-tuple-element.457, f32[16,8,64,64]{3,2,1,0:T(8,128)} %multiply_reduce_fusion.37, f32[16,8]{1,0:T(8,128)S(1)} %compare_convert_fusion.5, f32[16,8,32,64]{3,2,1,0:T(8,128)} %bitcast.468, ...), kind=kOutput, calls=%fused_computation.38.clone.1 | convolution fusion | flops 203161600 | bytes 6554752 | tf_op jit(solution)/shard_map/while/body/eval_jaxpr/wspq,rwsq->rwp/dot_general | solution.py:115
  408.6 3.7 multiply_reduce_fusion.37
  412.3 4.8 gather_fusion.4
  417.0 8.9 %fusion.286 = f32[8,32,16,64]{3,1,2,0:T(8,128)} fusion(f32[8,32,16,64]{3,1,2,0:T(8,128)} %get-tuple-element.458, s32[]{:T(128)} %get-tuple-element.457, f32[16,8,64,64]{3,2,1,0:T(8,128)} %multiply_reduce_fusion.37, f32[16,8]{1,0:T(8,128)S(1)} %compare_convert_fusion.5, f32[16,8,32,64]{3,2,1,0:T(8,128)} %bitcast.468, ...), kind=kOutput, calls=%fused_computation.38.clone.1 | convolution fusion | flops 203161600 | bytes 6554752 | tf_op jit(solution)/shard_map/while/body/eval_jaxpr/wspq,rwsq->rwp/dot_general | solution.py:115
  431.4 3.7 multiply_reduce_fusion.37
  435.1 4.8 gather_fusion.4
  439.8 8.9 %fusion.286 = f32[8,32,16,64]{3,1,2,0:T(8,128)} fusion(f32[8,32,16,64]{3,1,2,0:T(8,128)} %get-tuple-element.458, s32[]{:T(128)} %get-tuple-element.457, f32[16,8,64,64]{3,2,1,0:T(8,128)} %multiply_reduce_fusion.37, f32[16,8]{1,0:T(8,128)S(1)} %compare_convert_fusion.5, f32[16,8,32,64]{3,2,1,0:T(8,128)} %bitcast.468, ...), kind=kOutput, calls=%fused_computation.38.clone.1 | convolution fusion | flops 203161600 | bytes 6554752 | tf_op jit(solution)/shard_map/while/body/eval_jaxpr/wspq,rwsq->rwp/dot_general | solution.py:115
  454.2 3.7 multiply_reduce_fusion.37
  457.9 4.8 gather_fusion.4
  462.6 8.9 %fusion.286 = f32[8,32,16,64]{3,1,2,0:T(8,128)} fusion(f32[8,32,16,64]{3,1,2,0:T(8,128)} %get-tuple-element.458, s32[]{:T(128)} %get-tuple-element.457, f32[16,8,64,64]{3,2,1,0:T(8,128)} %multiply_reduce_fusion.37, f32[16,8]{1,0:T(8,128)S(1)} %compare_convert_fusion.5, f32[16,8,32,64]{3,2,1,0:T(8,128)} %bitcast.468, ...), kind=kOutput, calls=%fused_computation.38.clone.1 | convolution fusion | flops 203161600 | bytes 6554752 | tf_op jit(solution)/shard_map/while/body/eval_jaxpr/wspq,rwsq->rwp/dot_general | solution.py:115
  477.0 3.7 multiply_reduce_fusion.37
  480.7 4.8 gather_fusion.4
  485.4 8.9 %fusion.286 = f32[8,32,16,64]{3,1,2,0:T(8,128)} fusion(f32[8,32,16,64]{3,1,2,0:T(8,128)} %get-tuple-element.458, s32[]{:T(128)} %get-tuple-element.457, f32[16,8,64,64]{3,2,1,0:T(8,128)} %multiply_reduce_fusion.37, f32[16,8]{1,0:T(8,128)S(1)} %compare_convert_fusion.5, f32[16,8,32,64]{3,2,1,0:T(8,128)} %bitcast.468, ...), kind=kOutput, calls=%fused_computation.38.clone.1 | convolution fusion | flops 203161600 | bytes 6554752 | tf_op jit(solution)/shard_map/while/body/eval_jaxpr/wspq,rwsq->rwp/dot_general | solution.py:115
  494.3 3.3 copy_bitcast_fusion
  497.6 166.5 %while.20 = (s32[]{:T(128)}, f32[8,32,16,128]{3,1,2,0:T(8,128)}, s32[8]{0:T(128)S(1)}, s32[128,8]{0,1:T(8,128)S(1)}, bf16[32,384,128]{2,0,1:T(8,128)(2,1)}, /*in...) while((s32[]{:T(128)}, f32[8,32,16,128]{3,1,2,0:T(8,128)}, ...), condition=%wide.region_2.3_spmd, body=%wide.region_0.2_spmd.sunk | while | flops 160090880 | bytes 21778472 | solution.py:133
  503.6 5.7 multiply_reduce_fusion.36
  511.9 6.7 %fusion.282 = f32[8,32,16,128]{3,1,2,0:T(8,128)} fusion(f32[8,32,16,128]{3,1,2,0:T(8,128)} %get-tuple-element.495, s32[]{:T(128)} %get-tuple-element.494, f32[16,8,128,128]{3,2,1,0:T(8,128)} %multiply_reduce_fusion.36, f32[16,8]{1,0:T(8,128)S(1)} %get-tuple-element.431, bf16[16,8,32,128]{3,2,1,0:T(8,128)(2,1)S(1)} %bitcast.472, ...), kind=kOutput, calls=%fused_computation.11.clone.1 | convolution fusion | flops 143261696 | bytes 9831556 | tf_op jit(solution)/shard_map/while/body/eval_jaxpr/wspq,rwsq->rwp/dot_general | solution.py:127
  524.4 5.7 multiply_reduce_fusion.36
  532.7 6.7 %fusion.282 = f32[8,32,16,128]{3,1,2,0:T(8,128)} fusion(f32[8,32,16,128]{3,1,2,0:T(8,128)} %get-tuple-element.495, s32[]{:T(128)} %get-tuple-element.494, f32[16,8,128,128]{3,2,1,0:T(8,128)} %multiply_reduce_fusion.36, f32[16,8]{1,0:T(8,128)S(1)} %get-tuple-element.431, bf16[16,8,32,128]{3,2,1,0:T(8,128)(2,1)S(1)} %bitcast.472, ...), kind=kOutput, calls=%fused_computation.11.clone.1 | convolution fusion | flops 143261696 | bytes 9831556 | tf_op jit(solution)/shard_map/while/body/eval_jaxpr/wspq,rwsq->rwp/dot_general | solution.py:127
  545.1 5.7 multiply_reduce_fusion.36
  553.4 6.7 %fusion.282 = f32[8,32,16,128]{3,1,2,0:T(8,128)} fusion(f32[8,32,16,128]{3,1,2,0:T(8,128)} %get-tuple-element.495, s32[]{:T(128)} %get-tuple-element.494, f32[16,8,128,128]{3,2,1,0:T(8,128)} %multiply_reduce_fusion.36, f32[16,8]{1,0:T(8,128)S(1)} %get-tuple-element.431, bf16[16,8,32,128]{3,2,1,0:T(8,128)(2,1)S(1)} %bitcast.472, ...), kind=kOutput, calls=%fused_computation.11.clone.1 | convolution fusion | flops 143261696 | bytes 9831556 | tf_op jit(solution)/shard_map/while/body/eval_jaxpr/wspq,rwsq->rwp/dot_general | solution.py:127
  565.9 5.7 multiply_reduce_fusion.36
  574.2 6.7 %fusion.282 = f32[8,32,16,128]{3,1,2,0:T(8,128)} fusion(f32[8,32,16,128]{3,1,2,0:T(8,128)} %get-tuple-element.495, s32[]{:T(128)} %get-tuple-element.494, f32[16,8,128,128]{3,2,1,0:T(8,128)} %multiply_reduce_fusion.36, f32[16,8]{1,0:T(8,128)S(1)} %get-tuple-element.431, bf16[16,8,32,128]{3,2,1,0:T(8,128)(2,1)S(1)} %bitcast.472, ...), kind=kOutput, calls=%fused_computation.11.clone.1 | convolution fusion | flops 143261696 | bytes 9831556 | tf_op jit(solution)/shard_map/while/body/eval_jaxpr/wspq,rwsq->rwp/dot_general | solution.py:127
  586.7 5.7 multiply_reduce_fusion.36
  595.0 6.7 %fusion.282 = f32[8,32,16,128]{3,1,2,0:T(8,128)} fusion(f32[8,32,16,128]{3,1,2,0:T(8,128)} %get-tuple-element.495, s32[]{:T(128)} %get-tuple-element.494, f32[16,8,128,128]{3,2,1,0:T(8,128)} %multiply_reduce_fusion.36, f32[16,8]{1,0:T(8,128)S(1)} %get-tuple-element.431, bf16[16,8,32,128]{3,2,1,0:T(8,128)(2,1)S(1)} %bitcast.472, ...), kind=kOutput, calls=%fused_computation.11.clone.1 | convolution fusion | flops 143261696 | bytes 9831556 | tf_op jit(solution)/shard_map/while/body/eval_jaxpr/wspq,rwsq->rwp/dot_general | solution.py:127
  607.5 5.7 multiply_reduce_fusion.36
  615.8 6.7 %fusion.282 = f32[8,32,16,128]{3,1,2,0:T(8,128)} fusion(f32[8,32,16,128]{3,1,2,0:T(8,128)} %get-tuple-element.495, s32[]{:T(128)} %get-tuple-element.494, f32[16,8,128,128]{3,2,1,0:T(8,128)} %multiply_reduce_fusion.36, f32[16,8]{1,0:T(8,128)S(1)} %get-tuple-element.431, bf16[16,8,32,128]{3,2,1,0:T(8,128)(2,1)S(1)} %bitcast.472, ...), kind=kOutput, calls=%fused_computation.11.clone.1 | convolution fusion | flops 143261696 | bytes 9831556 | tf_op jit(solution)/shard_map/while/body/eval_jaxpr/wspq,rwsq->rwp/dot_general | solution.py:127
  628.3 5.7 multiply_reduce_fusion.36
  636.6 6.7 %fusion.282 = f32[8,32,16,128]{3,1,2,0:T(8,128)} fusion(f32[8,32,16,128]{3,1,2,0:T(8,128)} %get-tuple-element.495, s32[]{:T(128)} %get-tuple-element.494, f32[16,8,128,128]{3,2,1,0:T(8,128)} %multiply_reduce_fusion.36, f32[16,8]{1,0:T(8,128)S(1)} %get-tuple-element.431, bf16[16,8,32,128]{3,2,1,0:T(8,128)(2,1)S(1)} %bitcast.472, ...), kind=kOutput, calls=%fused_computation.11.clone.1 | convolution fusion | flops 143261696 | bytes 9831556 | tf_op jit(solution)/shard_map/while/body/eval_jaxpr/wspq,rwsq->rwp/dot_general | solution.py:127
  649.0 5.7 multiply_reduce_fusion.36
  657.3 6.7 %fusion.282 = f32[8,32,16,128]{3,1,2,0:T(8,128)} fusion(f32[8,32,16,128]{3,1,2,0:T(8,128)} %get-tuple-element.495, s32[]{:T(128)} %get-tuple-element.494, f32[16,8,128,128]{3,2,1,0:T(8,128)} %multiply_reduce_fusion.36, f32[16,8]{1,0:T(8,128)S(1)} %get-tuple-element.431, bf16[16,8,32,128]{3,2,1,0:T(8,128)(2,1)S(1)} %bitcast.472, ...), kind=kOutput, calls=%fused_computation.11.clone.1 | convolution fusion | flops 143261696 | bytes 9831556 | tf_op jit(solution)/shard_map/while/body/eval_jaxpr/wspq,rwsq->rwp/dot_general | solution.py:127
  664.1 2.9 fusion.36
  (547 shorter events, 219.8 us)
Async XLA Ops:
  0.0 9.9 %copy-start = (bf16[128,64,128]{2,1,0:T(8,128)(2,1)S(1)}, bf16[128,64,128]{2,1,0:T(8,128)(2,1)}, u32[]{:S(2)}) copy-start(bf16[128,64,128]{2,1,0:T(8,128)(2,1)} %param.12) | copy-start | bytes 6291460
  0.0 27.1 %copy-start.1 = (f32[2,64,64]{2,1,0:T(8,128)S(1)}, f32[2,64,64]{2,1,0:T(8,128)}, u32[]{:S(2)}) copy-start(f32[2,64,64]{2,1,0:T(8,128)} %param.13) | copy-start | bytes 98308
  0.0 282.0 %collective-permute-start.2 = (f32[3,16384]{1,0:T(4,128)}, f32[3,16384]{1,0:T(4,128)}, u32[]{:S(2)}, u32[]{:S(2)}) collective-permute-start(f32[3,16384]{1,0:T(4,128)} %param.11), channel_id=1, source_target_pairs={{0,1},{1,2},{2,3},{3,4},{4,5},{5,6},{6,7},{7,8},{8,9},{9,10},{10,1... | collective-permute-start | bytes 589832 | tf_op jit(solution)/shard_map/ppermute | solution.py:24
  2.1 287.8 %collective-permute-start.3 = (f32[3,16384]{1,0:T(4,128)}, f32[3,16384]{1,0:T(4,128)}, u32[]{:S(2)}, u32[]{:S(2)}) collective-permute-start(f32[3,16384]{1,0:T(4,128)} %param.11), channel_id=1, source_target_pairs={{1,0},{2,1},{3,2},{4,3},{5,4},{6,5},{7,6},{8,7},{9,8},{10,9},{11,1... | collective-permute-start | bytes 589832 | tf_op jit(solution)/shard_map/ppermute | solution.py:27
  17.4 279.9 %collective-permute-start.11 = (f32[32,128,64]{1,2,0:T(8,128)}, f32[32,128,64]{1,2,0:T(8,128)}, u32[]{:S(2)}, u32[]{:S(2)}) collective-permute-start(f32[32,128,64]{1,2,0:T(8,128)} %copy.231), channel_id=1, source_target_pairs={{0,1},{1,2},{2,3},{3,4},{4,5},{5,6},{6,7},{7,8},{8,9},{9,10},{10,1... | collective-permute-start | bytes 3145736 | tf_op jit(solution)/shard_map/ppermute | solution.py:24
  19.3 282.1 %collective-permute-start.12 = (f32[32,128,64]{1,2,0:T(8,128)}, f32[32,128,64]{1,2,0:T(8,128)}, u32[]{:S(2)}, u32[]{:S(2)}) collective-permute-start(f32[32,128,64]{1,2,0:T(8,128)} %copy.231), channel_id=1, source_target_pairs={{1,0},{2,1},{3,2},{4,3},{5,4},{6,5},{7,6},{8,7},{9,8},{10,9},{11,1... | collective-permute-start | bytes 3145736 | tf_op jit(solution)/shard_map/ppermute | solution.py:27
  27.2 11.1 %copy-start.5 = (f32[3,16384]{1,0:T(4,128)S(1)}, f32[3,16384]{1,0:T(4,128)}, u32[]{:S(2)}) copy-start(f32[3,16384]{1,0:T(4,128)} %param.11) | copy-start | bytes 589828
  32.8 0.8 copy-start.3
  34.5 0.7 copy-start.7
  35.6 0.7 copy-start.11
  36.8 0.6 copy-start.14
  38.2 186.0 %collective-permute-start.4 = (f32[32,64]{1,0:T(8,128)}, f32[32,64]{1,0:T(8,128)}, u32[]{:S(2)}, u32[]{:S(2)}) collective-permute-start(f32[32,64]{1,0:T(8,128)} %convolution_bitcast_fusion.18), channel_id=1, source_target_pairs={{0,1},{1,0},{2,3},{3,2},{4,5},{5,4},{6,7},{7,6},{8,9},{9,8},{10,11... | collective-permute-start | bytes 24584 | tf_op jit(solution)/shard_map/ppermute | solution.py:35
  38.9 6.4 copy-start.16
  41.7 126.3 %copy-start.12 = (f32[32,8,64,1]{2,0,3,1:T(8,128)S(1)}, f32[32,8,64,1]{2,0,3,1:T(8,128)}, u32[]{:S(2)}) copy-start(f32[32,8,64,1]{2,0,3,1:T(8,128)} %copy-done.11) | copy-start | bytes 196612
  41.9 2.1 copy-start.34
  45.8 0.6 copy-start.23
  46.5 4.1 copy-start.22
  46.6 4.0 copy-start.25
  46.7 3.9 copy-start.28
  46.9 3.7 copy-start.37
  47.0 3.6 copy-start.29
  47.0 3.6 copy-start.38
  162.1 15.9 %copy-start.27 = (f32[3,16,2]{1,0,2:T(4,128)S(1)}, f32[3,16,2]{1,0,2:T(4,128)}, u32[]{:S(2)}) copy-start(f32[3,16,2]{1,0,2:T(4,128)} %copy.217) | copy-start | bytes 1156
  162.1 15.9 %copy-start.31 = (f32[16,2]{0,1:T(2,128)S(1)}, f32[16,2]{0,1:T(2,128)}, u32[]{:S(2)}) copy-start(f32[16,2]{0,1:T(2,128)} %copy.218) | copy-start | bytes 388
  174.5 3.6 copy-start.4
  175.5 6.8 %copy-start.30 = (f32[3,2,1]{0,2,1:T(1,128)S(1)}, f32[3,2,1]{0,2,1:T(1,128)}, u32[]{:S(2)}) copy-start(f32[3,2,1]{0,2,1:T(1,128)} %copy-done.29) | copy-start | bytes 76
  175.5 7.5 %copy-start.36 = (f32[64]{0:T(128)S(1)}, f32[64]{0:T(128)}, u32[]{:S(2)}) copy-start(f32[64]{0:T(128)} %get-tuple-element.303) | copy-start | bytes 772
  178.0 18.8 %copy-start.9 = (f32[32,32,64]{2,1,0:T(8,128)S(1)}, f32[32,32,64]{2,1,0:T(8,128)}, u32[]{:S(2)}) copy-start(f32[32,32,64]{2,1,0:T(8,128)} %get-tuple-element.245) | copy-start | bytes 786436
  182.4 21.1 %copy-start.32 = (s32[128,8]{0,1:T(8,128)S(1)}, s32[128,8]{0,1:T(8,128)}, u32[]{:S(2)}) copy-start(s32[128,8]{0,1:T(8,128)} %param.15) | copy-start | bytes 12292
  182.4 21.1 %copy-start.33 = (s32[128,8]{0,1:T(8,128)S(1)}, s32[128,8]{0,1:T(8,128)}, u32[]{:S(2)}) copy-start(s32[128,8]{0,1:T(8,128)} %param.14) | copy-start | bytes 12292
  183.6 13.2 %copy-start.26 = (f32[3,32]{1,0:T(4,128)}, f32[3,32]{1,0:T(4,128)S(1)}, u32[]{:S(2)}) copy-start(f32[3,32]{1,0:T(4,128)S(1)} %get-tuple-element.167) | copy-start | bytes 1156
  185.5 8.9 %copy-start.24 = (f32[3,16]{1,0:T(4,128)}, f32[3,16]{1,0:T(4,128)S(1)}, u32[]{:S(2)}) copy-start(f32[3,16]{1,0:T(4,128)S(1)} %get-tuple-element.171) | copy-start | bytes 580
  195.3 51.2 %copy-start.15 = (f32[32,2,64,1]{2,0,3,1:T(8,128)S(1)}, f32[32,2,64,1]{2,0,3,1:T(8,128)}, u32[]{:S(2)}) copy-start(f32[32,2,64,1]{2,0,3,1:T(8,128)} %copy-done.14) | copy-start | bytes 49156
  199.9 62.5 %copy-start.2 = (bf16[32,16384]{1,0:T(8,128)(2,1)S(1)}, bf16[32,16384]{1,0:T(8,128)(2,1)}, u32[]{:S(2)}) copy-start(bf16[32,16384]{1,0:T(8,128)(2,1)} %param.10) | copy-start | bytes 3145732
  199.9 72.6 %copy-start.18 = (f32[32,2,1,64]{3,0,2,1:T(8,128)S(1)}, f32[32,2,1,64]{3,0,2,1:T(8,128)}, u32[]{:S(2)}) copy-start(f32[32,2,1,64]{3,0,2,1:T(8,128)} %convolution_bitcast_fusion.9) | copy-start | bytes 49156
  199.9 72.6 %copy-start.19 = (f32[32,2,1,64]{3,0,2,1:T(8,128)S(1)}, f32[32,2,1,64]{3,0,2,1:T(8,128)}, u32[]{:S(2)}) copy-start(f32[32,2,1,64]{3,0,2,1:T(8,128)} %convolution_bitcast_fusion.8) | copy-start | bytes 49156
  203.5 70.6 %copy-start.13 = (f32[32,8,1,64]{3,0,2,1:T(8,128)S(1)}, f32[32,8,1,64]{3,0,2,1:T(8,128)}, u32[]{:S(2)}) copy-start(f32[32,8,1,64]{3,0,2,1:T(8,128)} %convolution_bitcast_fusion.4) | copy-start | bytes 196612
  225.8 4.1 collective-permute-start.5
  231.4 5.6 collective-permute-start.6
  238.6 4.1 collective-permute-start.7
  244.2 5.6 collective-permute-start.8
  251.3 4.1 collective-permute-start.9
  252.1 20.1 %copy-start.20 = (f32[32,1,1,64]{3,0,2,1:T(8,128)S(1)}, f32[32,1,1,64]{3,0,2,1:T(8,128)}, u32[]{:S(2)}) copy-start(f32[32,1,1,64]{3,0,2,1:T(8,128)} %convolution_bitcast_fusion.11) | copy-start | bytes 24580
  252.1 20.1 %copy-start.21 = (f32[32,1,1,64]{3,0,2,1:T(8,128)S(1)}, f32[32,1,1,64]{3,0,2,1:T(8,128)}, u32[]{:S(2)}) copy-start(f32[32,1,1,64]{3,0,2,1:T(8,128)} %convolution_bitcast_fusion.10) | copy-start | bytes 24580
  256.9 5.5 collective-permute-start.10
  262.4 231.9 %collective-permute-start = (bf16[32,16384]{1,0:T(8,128)(2,1)S(1)}, bf16[32,16384]{1,0:T(8,128)(2,1)}, u32[]{:S(2)}, u32[]{:S(2)}) collective-permute-start(bf16[32,16384]{1,0:T(8,128)(2,1)S(1)} %copy-done.2), channel_id=1, source_target_pairs={{0,1},{1,2},{2,3},{3,4},{4,5},{5,6},{6,7},{7,8},{8,9},{9,10},{10,1... | collective-permute-start | bytes 3145736 | tf_op jit(solution)/shard_map/ppermute | solution.py:24
  278.2 11.6 %copy-start.6 = (f32[3,16384]{1,0:T(4,128)S(1)}, f32[3,16384]{1,0:T(4,128)}, u32[]{:S(2)}) copy-start(f32[3,16384]{1,0:T(4,128)} %param.11) | copy-start | bytes 589828
  278.8 15.2 %copy-start.10 = (f32[3,128,128]{2,1,0:T(8,128)S(1)}, f32[3,128,128]{2,1,0:T(8,128)}, u32[]{:S(2)}) copy-start(f32[3,128,128]{2,1,0:T(8,128)} %get-tuple-element.488) | copy-start | bytes 589828
  282.0 212.4 %collective-permute-start.1 = (bf16[32,16384]{1,0:T(8,128)(2,1)S(1)}, bf16[32,16384]{1,0:T(8,128)(2,1)}, u32[]{:S(2)}, u32[]{:S(2)}) collective-permute-start(bf16[32,16384]{1,0:T(8,128)(2,1)S(1)} %copy-done.2), channel_id=1, source_target_pairs={{1,0},{2,1},{3,2},{4,3},{5,4},{6,5},{7,6},{8,7},{9,8},{10,9},{11,1... | collective-permute-start | bytes 3145736 | tf_op jit(solution)/shard_map/ppermute | solution.py:27
  305.4 6.3 copy-start.17
  305.4 6.3 copy-start.35
  305.4 6.3 copy-start.39
  664.1 2.9 copy-start.8
where the time goes:
time: 682 us; the launch traced here: 670 us
  matrix products  179 us (26%)
  local copies, waits for them, and re-layouts  157 us (23%)
  other arithmetic  157 us (23%)
  blocking collectives  93.1 us (14%)
  starting transfers between devices  35.5 us (5%)
  loops' own time  31.6 us (5%)
  waiting for transfers between devices  13.8 us (2%)
    reduce_sum x29, other arithmetic, covariance(): jnp.sum(separation * separation, axis=0)  85 us
    dot_general x8, matrix products, listed_coupling(): jnp.einsum('wspq,rwsq->rwp', kernel_tile, far_coef, precision=HIGHEST)  71.1 us
    unnamed x1, blocking collectives  64 us
    dot_general x8, matrix products, near_tile(): jnp.einsum('wspq,rwsq->rwp', kernel_tile, far_x, preferred_element_type=j...  53.9 us
    gather x8, local copies, waits for them, and re-layouts, listed_coupling(): far_coef = jnp.take(all_coef, safe_rows, axis=1)  38.2 us
    another operation x2, loops' own time, blocked(): pieces = lax.map(function, starts)  31.6 us
    all_gather x1, blocking collectives, per_device(): lax.all_gather(levels[-1][1], ('leaf', 'sub'), axis=1, tiled=True)  29.1 us
    ppermute x3, starting transfers between devices, padded(): lax.ppermute(lax.slice_in_dim(block, 0, width, axis=dim), axis, backward)  23.6 us
  transfers between devices with their start and end apart: 13, of which 6 were waited for; matrix products, arithmetic and copies ran while one was open for 49% of the time, Pallas kernels for 0%

commit v1 on v0

v1 whole, which is shorter than its diff:
```python
import math

import jax
import jax.numpy as jnp
from jax import lax
from jax.experimental import pallas as pl
from jax.experimental.pallas import tpu as pltpu
from jax.sharding import PartitionSpec as P

F32, BF16 = jnp.float32, jnp.bfloat16
PT = 128
K = 64
R = 32
LD = 128
REACH = 64
GRP = 4
GW = GRP * PT
GROUPS = LD // GRP
EXT = (GROUPS + 2) * GW
FEAT = 48
SCALE = math.log2(math.e) / 2.0
TINY = 1e-30
MESH = pl.DeviceIdType.MESH


def dot(a, b):
    return lax.dot_general(a, b, (((1,), (0,)), ((), ())), preferred_element_type=F32)


def dot_nt(a, b):
    return lax.dot_general(a, b, (((1,), (1,)), ((), ())), preferred_element_type=F32)


def dot_tn(a, b):
    return lax.dot_general(a, b, (((0,), (0,)), ((), ())), preferred_element_type=F32)


def split2(x):
    high = x.astype(BF16)
    return high, (x - high.astype(F32)).astype(BF16)


def dot3(a, b_high, b_low):
    high, low = split2(a)
    return dot(high, b_high) + (dot(high, b_low) + dot(low, b_high))


def from_square(d2):
    x = jnp.maximum(d2, TINY)
    return jnp.exp2(-(x * lax.rsqrt(x)))


def features(coords, axis):
    high = coords.astype(BF16).astype(F32)
    low = (coords - high).astype(BF16).astype(F32)
    kept = high + low
    norm = jnp.sum(kept * kept, axis=axis, keepdims=True)
    n1 = norm.astype(BF16).astype(F32)
    n2 = (norm - n1).astype(BF16).astype(F32)
    n3 = norm - n1 - n2
    row = lax.broadcasted_iota(jnp.int32, coords.shape, axis)
    norms = jnp.where(row == 0, n1, jnp.where(row == 1, n2, jnp.where(row == 2, n3, 0.0)))
    ones = jnp.where(row < 3, 1.0, 0.0)
    high2, low2 = -2.0 * high, -2.0 * low
    u = jnp.concatenate([high, high, low, low, norms, ones], axis=axis)
    v = jnp.concatenate([high2, low2, high2, low2, ones, norms], axis=axis)
    return u, v


def unit_rows():
    row = lax.broadcasted_iota(jnp.int32, (8, 128), 0)
    index = lax.broadcasted_iota(jnp.int32, (8, 128), 1) % K
    digit = jnp.where(row == 0, index // 16, jnp.where(row == 1, index // 4 % 4, index % 4))
    big, small = math.cos(math.pi / 8.0), math.cos(3.0 * math.pi / 8.0)
    value = jnp.where(
        digit == 0, big, jnp.where(digit == 1, small, jnp.where(digit == 2, -small, -big))
    )
    return jnp.where(row < 3, value, 0.0).astype(F32)


def lower_lanes(shape):
    return lax.broadcasted_iota(jnp.int32, shape, len(shape) - 1) < K


def halves(x):
    paired = x.reshape((x.shape[0] // 2, 2) + x.shape[1:])
    return paired[:, 0], paired[:, 1]


def side_by_side(x):
    left, right = halves(x)
    return jnp.where(lower_lanes(left.shape), left, right)


def merge_shapes(centers, radii):
    c0, c1 = halves(centers)
    r0, r1 = halves(radii)
    gap = c0 - c1
    reach = jnp.sqrt(jnp.sum(gap * gap, axis=1, keepdims=True))
    return 0.5 * (c0 + c1), jnp.maximum(r0, r1) + 0.5 * reach


def pair_coords(centers, radii, units):
    c0, c1 = halves(centers)
    r0, r1 = halves(radii)
    half = 0.5 * (c0 - c1)
    left = lower_lanes(half.shape)
    return SCALE * (jnp.where(left, half, -half) + jnp.where(left, r0, r1) * units[None])


def couple_pair(coefs, coords):
    columns = jnp.transpose(coords)
    d2 = None
    for k in range(3):
        gap = columns[:, k : k + 1] - coords[k : k + 1, :]
        d2 = gap * gap if d2 is None else d2 + gap * gap
    across = (lax.broadcasted_iota(jnp.int32, (128, 128), 0) < K) != lower_lanes((128, 128))
    tile = jnp.where(across, from_square(d2), 0.0)
    tile_high, tile_low = split2(tile)
    return dot3(coefs, tile_high, tile_low)


def kernel(
    nl, ns,
    charges, points, basis, transfer, near_list, coupling_list,
    out,
    p8, xe, oe, ua, va, vb, weight,
    leaf_pts, centers, radii, pairs, pair_co, sib,
    up_pair, v_left, v_right, c_left, c_right, lc,
    send_coef, halo_coef, send_shape, halo_shape,
    root, got_sub, root_b, got_leaf, path_pair, path_co, e0,
    near_send, near_recv, coup_send, coup_recv, sub_send, sub_recv, leaf_send, leaf_recv,
):
    leaf_id, sub_id = lax.axis_index("leaf"), lax.axis_index("sub")
    count = nl * ns
    me = leaf_id * ns + sub_id
    right, left = lax.rem(me + 1, count), lax.rem(me + count - 1, count)
    left_dev = (left // ns, lax.rem(left, ns))
    right_dev = (right // ns, lax.rem(right, ns))
    sub_devs = [(leaf_id, lax.rem(sub_id + o, ns)) for o in range(1, ns)]
    leaf_devs = [(lax.rem(leaf_id + o, nl), sub_id) for o in range(1, nl)]
    barrier = pltpu.get_barrier_semaphore()
    partners = [left_dev, right_dev] + sub_devs + leaf_devs
    for device in partners:
        pl.semaphore_signal(barrier, inc=1, device_id=device, device_id_type=MESH)

    def send(src, dst, send_sem, recv_sem, device):
        copy = pltpu.make_async_remote_copy(
            src_ref=src, dst_ref=dst, send_sem=send_sem, recv_sem=recv_sem,
            device_id=device, device_id_type=MESH,
        )
        copy.start()
        return copy

    first = me * LD
    units = unit_rows()
    lane_half = lower_lanes((R, 128))

    p8[3:8, GW : EXT - GW] = jnp.zeros((5, LD * PT), F32)
    p8[0:3, GW : EXT - GW] = points[...]

    pl.semaphore_wait(barrier, len(partners))
    copies = []
    copies.append(send(charges.at[:, pl.ds(0, GW)], xe.at[:, pl.ds(EXT - GW, GW)],
                       near_send.at[0], near_recv.at[0], left_dev))
    copies.append(send(charges.at[:, pl.ds(LD * PT - GW, GW)], xe.at[:, pl.ds(0, GW)],
                       near_send.at[1], near_recv.at[1], right_dev))
    copies.append(send(p8.at[:, pl.ds(GW, GW)], p8.at[:, pl.ds(EXT - GW, GW)],
                       near_send.at[2], near_recv.at[2], left_dev))
    copies.append(send(p8.at[:, pl.ds(EXT - 2 * GW, GW)], p8.at[:, pl.ds(0, GW)],
                       near_send.at[3], near_recv.at[3], right_dev))
    near_copies = copies

    for c in range(LD):
        leaf_pts[c] = p8[:, GW + c * PT : GW + (c + 1) * PT]

    @pl.loop(0, LD // 16)
    def _(block):
        rows = pl.ds(block * 16, 16)
        pts = leaf_pts[rows]
        center = jnp.mean(pts, axis=2, keepdims=True)
        off = pts - center
        far = jnp.max(jnp.sum(off * off, axis=1, keepdims=True), axis=2, keepdims=True)
        centers[rows] = jnp.broadcast_to(center, pts.shape)
        radii[rows] = jnp.broadcast_to(jnp.sqrt(far), pts.shape)

    row8 = lax.broadcasted_iota(jnp.int32, (8, 128), 0)
    lane8 = lax.broadcasted_iota(jnp.int32, (8, 128), 1)

    packed = jnp.zeros((8, 128), F32)
    for c in range(LD):
        packed = jnp.where(lane8 == c, jnp.where(row8 < 3, centers[c], radii[c]), packed)
    send_shape[...] = packed

    @pl.loop(0, LD // 16)
    def _(block):
        for s in range(8):
            m = block * 8 + s
            x = charges[:, pl.ds(pl.multiple_of(m * 256, 256), 256)]
            stacked = jnp.concatenate([x[:, :128], x[:, 128:]], axis=0)
            both = basis[pl.ds(2 * m, 2)].reshape(2 * K, PT)
            product = dot_nt(stacked, both)
            pair = jnp.where(lane_half, product[:R], product[R:])
            pairs[m] = pair
            send_coef[m] = pair.astype(BF16)

    half_pairs = REACH // 2
    coup_copies = [
        send(send_coef.at[pl.ds(0, half_pairs)], halo_coef.at[1],
             coup_send.at[0], coup_recv.at[0], left_dev),
        send(send_coef.at[pl.ds(half_pairs, half_pairs)], halo_coef.at[0],
             coup_send.at[1], coup_recv.at[1], right_dev),
        send(send_shape, halo_shape.at[1], coup_send.at[2], coup_recv.at[2], left_dev),
        send(send_shape, halo_shape.at[0], coup_send.at[3], coup_recv.at[3], right_dev),
    ]

    t0, t1 = transfer[0], transfer[1]
    up = jnp.concatenate([t0, t1], axis=0)
    up_high, up_low = split2(jnp.concatenate([up, up], axis=1))
    down = jnp.concatenate([jnp.transpose(t0), jnp.transpose(t1)], axis=1)
    down_high, down_low = split2(jnp.concatenate([down, down], axis=0))

    def lift(pair_block):
        n = pair_block.shape[0]
        return dot3(pair_block.reshape(n * R, 128), up_high, up_low).reshape(n, R, 128)

    level_cen, level_rad = centers[...], radii[...]
    offset, n = 0, LD // 2
    block = pairs[pl.ds(0, n)]
    while n > 1:
        block = side_by_side(lift(block))
        level_cen, level_rad = merge_shapes(level_cen, level_rad)
        offset += n
        n //= 2
        pairs[pl.ds(offset, n)] = block
        pair_co[pl.ds(offset - LD // 2, n)] = pair_coords(level_cen, level_rad, units)
    root_coef = lift(block)[0]
    root_cen, root_rad = merge_shapes(level_cen, level_rad)

    def packed_shape(cen, rad):
        return jnp.where(row8 < 3, cen, rad)

    def unpacked_shape(shape):
        rows = lax.broadcasted_iota(jnp.int32, shape.shape, 1)
        cen = jnp.where(rows < 3, shape, 0.0)
        rad = jnp.sum(jnp.where(rows == 3, shape, 0.0), axis=1, keepdims=True)
        return cen, jnp.broadcast_to(rad, shape.shape)

    root[0:R, :] = root_coef
    root[R : R + 8, :] = packed_shape(root_cen[0], root_rad[0])
    sub_copies = [
        send(root, got_sub.at[sub_id], sub_send.at[o], sub_recv.at[o], device)
        for o, device in enumerate(sub_devs)
    ]
    got_sub[sub_id] = root[...]

    @pl.loop(0, 21)
    def _(i):
        for s in range(3):
            sib[i * 3 + s] = couple_pair(pairs[LD // 2 + i * 3 + s], pair_co[i * 3 + s])

    xe[:, GW : EXT - GW] = charges[...]
    oe[:, GW : EXT - GW] = charges[...].astype(F32)
    leaf_row = lax.broadcasted_iota(jnp.int32, (LD, 1), 0)
    base = first + (leaf_row // GRP) * GRP - GRP
    listed = near_list[...]
    relative = jnp.where(listed >= 0, listed - base, -1)
    weight[...] = jnp.zeros_like(weight)
    for k in range(3 * GRP):
        times = jnp.sum(jnp.where(relative == k, 1.0, 0.0), axis=1, keepdims=True)
        weight[k, GRP : GRP + LD, :] = jnp.broadcast_to(times, (LD, 128))

    for copy in near_copies:
        copy.wait()

    @pl.loop(0, GROUPS + 2)
    def _(g):
        lanes = pl.ds(pl.multiple_of(g * GW, GW), GW)
        row = lax.broadcasted_iota(jnp.int32, (8, GW), 0)
        z0 = (me * GROUPS + g - 1).astype(F32)
        corner = jnp.where(row == 2, z0, jnp.where(row < 2, 1.0, 0.0))
        low = p8[:, lanes] - corner
        shift = jnp.where(row == 2, 1.0, 0.0)
        u, v = features(SCALE * (low - shift), 0)
        ua[:, lanes] = u.astype(BF16)
        va[:, lanes] = v.astype(BF16)
        vb[:, lanes] = features(SCALE * low, 0)[1].astype(BF16)

    oe[:, 0:GW] = jnp.zeros((R, GW), F32)
    oe[:, EXT - GW : EXT] = jnp.zeros((R, GW), F32)

    @pl.loop(0, GROUPS + 1)
    def _(g):
        here = pl.ds(pl.multiple_of(g * GW, GW), GW)
        there = pl.ds(pl.multiple_of(g * GW + GW, GW), GW)
        u = ua[:, here]
        v = jnp.concatenate([va[:, here], vb[:, there]], axis=1)
        x = jnp.concatenate([xe[:, here], xe[:, there]], axis=1)
        total = [oe[:, here][:, j * PT : (j + 1) * PT] for j in range(GRP)]
        total += [oe[:, there][:, j * PT : (j + 1) * PT] for j in range(GRP)]

        def times(target, source):
            k = source + GRP if target < GRP else source
            return weight[k, pl.ds(g * GRP + target, 1), :]

        for i in range(GRP):
            d2 = dot_tn(u[:, i * PT : (i + 1) * PT], v[:, i * PT :])
            tile = from_square(d2).astype(BF16)
            part = dot(x[:, i * PT : (i + 1) * PT], tile)
            for j in range(i, 2 * GRP):
                at = (j - i) * PT
                total[j] = total[j] + times(j, i) * part[:, at : at + PT]
                if j > i:
                    back = dot_nt(x[:, j * PT : (j + 1) * PT], tile[:, at : at + PT])
                    total[i] = total[i] + times(i, j) * back
        oe[:, here] = jnp.concatenate(total[:GRP], axis=1)
        oe[:, there] = jnp.concatenate(total[GRP:], axis=1)

    def climb(got, width, level0, index):
        coefs = got[:, 0:R, :]
        cen, rad = unpacked_shape(got[:, R : R + 8, :])
        level = level0
        while width > 1:
            two = side_by_side(coefs)
            path_pair[level, pl.ds(0, width // 2)] = two
            path_co[level, pl.ds(0, width // 2)] = pair_coords(cen, rad, units)
            coefs = lift(two)
            cen, rad = merge_shapes(cen, rad)
            width //= 2
            level += 1
        return coefs[0], packed_shape(cen[0], rad[0])

    sub_levels, leaf_levels = ns.bit_length() - 1, nl.bit_length() - 1
    for copy in sub_copies:
        copy.wait()
    top_coef, top_shape = climb(got_sub[...], ns, 0, sub_id)
    root_b[0:R, :] = top_coef
    root_b[R : R + 8, :] = top_shape
    leaf_copies = [
        send(root_b, got_leaf.at[leaf_id], leaf_send.at[o], leaf_recv.at[o], device)
        for o, device in enumerate(leaf_devs)
    ]
    got_leaf[leaf_id] = root_b[...]

    for copy in coup_copies:
        copy.wait()
    middle_row = lax.broadcasted_iota(jnp.int32, (1, 8, 128), 1)
    middle = jnp.where(
        middle_row == 2,
        (me * GROUPS + GROUPS // 2).astype(F32),
        jnp.where(middle_row < 2, 1.0, 0.0),
    )

    def put_leaves(where, cen, rad):
        u, v = features(SCALE * (cen - middle + rad * units[None]), 1)
        lower = lower_lanes(v.shape)
        v_left[pl.ds(where, 8)] = jnp.where(lower, v, 0.0).astype(BF16)
        v_right[pl.ds(where, 8)] = jnp.where(lower, 0.0, v).astype(BF16)
        return u

    def put_coefs(where, two):
        lower = lower_lanes((R, 128))
        first_left = jnp.where(lower, two, 0.0)
        second_right = jnp.where(lower, 0.0, two)
        c_left[where] = first_left.astype(BF16)
        c_right[where] = pltpu.roll(first_left, K, 1).astype(BF16)
        c_left[where + 1] = pltpu.roll(second_right, K, 1).astype(BF16)
        c_right[where + 1] = second_right.astype(BF16)

    @pl.loop(0, LD // 8)
    def _(b):
        u = put_leaves(REACH + b * 8, centers[pl.ds(b * 8, 8)], radii[pl.ds(b * 8, 8)])
        up_pair[pl.ds(b * 4, 4)] = side_by_side(u).astype(BF16)
        for s in range(4):
            put_coefs(REACH + b * 8 + 2 * s, pairs[b * 4 + s])

    for side, start, lane0 in ((0, 0, REACH), (1, REACH + LD, 0)):
        shape = halo_shape[side]
        for b in range(REACH // 8):
            cens, rads = [], []
            for s in range(8):
                lane = lane0 + b * 8 + s
                column = jnp.broadcast_to(shape[:, lane : lane + 1], (8, 128))
                cens.append(jnp.where(row8 < 3, column, 0.0))
                rads.append(jnp.broadcast_to(column[3:4, :], (8, 128)))
            put_leaves(start + b * 8, jnp.stack(cens), jnp.stack(rads))

        @pl.loop(0, REACH // 16)
        def _(b):
            for s in range(8):
                put_coefs(start + b * 16 + 2 * s, halo_coef[side, b * 8 + s].astype(F32))

    dead = LD + 2 * REACH
    for ref in (c_left, c_right, v_left, v_right):
        ref[dead] = jnp.zeros(ref.shape[1:], BF16)

    @pl.loop(0, LD // 2)
    def _(m):
        u = jnp.transpose(up_pair[m].astype(F32)).astype(BF16)
        tiles, sources = [], []
        for s in range(2):
            leaf = 2 * m + s
            vs, cs = [], []
            for t in range(4):
                picked = []
                for slot in (2 * t, 2 * t + 1):
                    j = coupling_list[leaf, slot]
                    near_by = jnp.clip(j - first + REACH, 0, dead - 1)
                    picked.append(jnp.where(j >= 0, near_by, dead))
                vs.append(v_left[picked[0]] + v_right[picked[1]])
                cs.append(c_left[picked[0]] + c_right[picked[1]])
            d2 = dot(u[s * K : (s + 1) * K], jnp.concatenate(vs, axis=1))
            tiles.append(from_square(d2).astype(BF16))
            sources.append(jnp.concatenate(cs, axis=1))
        product = dot_nt(jnp.concatenate(sources, axis=0), jnp.concatenate(tiles, axis=0))
        lc[m] = jnp.where(lane_half, product[:R], product[R:])

    for copy in leaf_copies:
        copy.wait()
    climb(got_leaf[...], nl, sub_levels, leaf_id)

    def masked(pair, side):
        chosen = lower_lanes(pair.shape) == (side == 0)
        return jnp.where(chosen, pair, 0.0)

    held = None
    for level in reversed(range(sub_levels + leaf_levels)):
        position = (sub_id if level < sub_levels else leaf_id)
        shift = level if level < sub_levels else level - sub_levels
        node = position // (2**shift)
        pair = node // 2
        mine = couple_pair(path_pair[level, pair], path_co[level, pair])
        if held is not None:
            mine = mine + dot3(held, down_high, down_low)
        held = masked(mine, lax.rem(node, 2))

    def spread(pair_block):
        n = pair_block.shape[0]
        lower = lower_lanes(pair_block.shape)
        both = jnp.stack(
            [jnp.where(lower, pair_block, 0.0), jnp.where(lower, 0.0, pair_block)], axis=1
        )
        return dot3(both.reshape(2 * n * R, 128), down_high, down_low).reshape(2 * n, R, 128)

    n, offset = 1, LD // 2 - 2
    block = sib[pl.ds(offset, 1)] + dot3(held, down_high, down_low)[None]
    while n < LD // 4:
        block = spread(block)
        n *= 2
        offset -= n
        block = block + sib[pl.ds(offset, n)]
    e0[...] = spread(block)

    @pl.loop(0, LD // 16)
    def _(b):
        for s in range(8):
            m = b * 8 + s
            coef = lc[m] + e0[m]
            stacked = jnp.concatenate(
                [jnp.where(lane_half, coef, 0.0), jnp.where(lane_half, 0.0, coef)], axis=0
            ).astype(BF16)
            far = dot(stacked, basis[pl.ds(2 * m, 2)].reshape(2 * K, PT))
            start = pl.multiple_of(m * 256, 256)
            near = oe[:, pl.ds(pl.multiple_of(GW + m * 256, 256), 256)]
            out[:, pl.ds(start, 256)] = near + jnp.concatenate([far[:R], far[R:]], axis=1)


def per_device(charges, points, basis, transfer, near_list, coupling_list):
    nl, ns = lax.axis_size("leaf"), lax.axis_size("sub")
    levels = (nl * ns).bit_length() - 1
    widest = max(nl, ns) // 2
    vmem = pl.BlockSpec(memory_space=pltpu.VMEM)
    total = LD + 2 * REACH + 1

    def body(*refs):
        kernel(nl, ns, *refs)

    dma = pltpu.SemaphoreType.DMA
    return pl.pallas_call(
        body,
        out_shape=jax.ShapeDtypeStruct((R, LD * PT), F32),
        in_specs=[vmem] * 5 + [pl.BlockSpec(memory_space=pltpu.SMEM)],
        out_specs=vmem,
        scratch_shapes=[
            pltpu.VMEM((8, EXT), F32),
            pltpu.VMEM((R, EXT), BF16),
            pltpu.VMEM((R, EXT), F32),
            pltpu.VMEM((FEAT, EXT), BF16),
            pltpu.VMEM((FEAT, EXT), BF16),
            pltpu.VMEM((FEAT, EXT), BF16),
            pltpu.VMEM((3 * GRP, LD + 2 * GRP, 128), F32),
            pltpu.VMEM((LD, 8, 128), F32),
            pltpu.VMEM((LD, 8, 128), F32),
            pltpu.VMEM((LD, 8, 128), F32),
            pltpu.VMEM((LD, R, 128), F32),
            pltpu.VMEM((LD // 2, 8, 128), F32),
            pltpu.VMEM((LD // 2, R, 128), F32),
            pltpu.VMEM((LD // 2, FEAT, 128), BF16),
            pltpu.VMEM((total, FEAT, 128), BF16),
            pltpu.VMEM((total, FEAT, 128), BF16),
            pltpu.VMEM((total, R, 128), BF16),
            pltpu.VMEM((total, R, 128), BF16),
            pltpu.VMEM((LD // 2, R, 128), F32),
            pltpu.VMEM((LD // 2, R, 128), BF16),
            pltpu.VMEM((2, REACH // 2, R, 128), BF16),
            pltpu.VMEM((8, 128), F32),
            pltpu.VMEM((2, 8, 128), F32),
            pltpu.VMEM((R + 8, 128), F32),
            pltpu.VMEM((ns, R + 8, 128), F32),
            pltpu.VMEM((R + 8, 128), F32),
            pltpu.VMEM((nl, R + 8, 128), F32),
            pltpu.VMEM((levels, widest, R, 128), F32),
            pltpu.VMEM((levels, widest, 8, 128), F32),
            pltpu.VMEM((LD // 2, R, 128), F32),
            dma((4,)), dma((4,)), dma((4,)), dma((4,)),
            dma((ns,)), dma((ns,)), dma((nl,)), dma((nl,)),
        ],
        compiler_params=pltpu.CompilerParams(
            collective_id=0, has_side_effects=True, vmem_limit_bytes=56 * 2**20
        ),
        cost_estimate=pl.CostEstimate(
            flops=6 * 10**9, bytes_accessed=7 * 10**6, transcendentals=4 * 10**7
        ),
    )(charges, points, basis, transfer, near_list, coupling_list)


def solution(mesh):
    in_specs = (
        P(None, ("leaf", "sub")),
        P(None, ("leaf", "sub")),
        P(("leaf", "sub"), None, None),
        P(),
        P(("leaf", "sub"), None),
        P(("leaf", "sub"), None),
    )
    return jax.shard_map(
        per_device,
        mesh=mesh,
        in_specs=in_specs,
        out_specs=P(None, ("leaf", "sub")),
        check_vma=False,
    )
```

time: 682 us -> 128 us (0.19)
  the two profiles are of different devices: /device:TPU:4 before, /device:TPU:0 now
where the time goes in v1:
time: 128 us
  Pallas kernels  122 us (95%)
  local copies, waits for them, and re-layouts  5.86 us (5%)
    pallas_call x1, Pallas kernels, per_device(): pl.pallas_call(body, out_shape=jax.ShapeDtypeStruct((R, LD * PT), F32), i...  122 us
    unnamed x3, local copies, waits for them, and re-layouts  5.86 us

profile of v1, /device:TPU:0, one launch (start us, length us, event | category | flops | bytes accessed | tf_op | source)
XLA Modules:
  0.0 127.7 jit_solution(3261663002621616811)
XLA Ops:
  0.0 1.4 %copy.7.refs_4_ = s32[128,8]{1,0:T(8,128)} copy(s32[128,8]{0,1:T(8,128)} %param.10) | data formatting | bytes 8192 | tf_op args[4]
  1.4 1.4 %copy.8.refs_5_ = s32[128,8]{1,0:T(8,128)} copy(s32[128,8]{0,1:T(8,128)} %param.11) | data formatting | bytes 8192 | tf_op args[5]
  2.8 121.8 %shard_map.64 = f32[32,16384]{1,0:T(8,128)} custom-call(bf16[32,16384]{1,0:T(8,128)(2,1)} %refs_0_.1, f32[3,16384]{1,0:T(4,128)} %refs_1_.1, bf16[128,64,128]{2,1,0:T(8,128)(2,1)} %refs_2_.1, f32[2,64,64]{2,1,0:T(8,128)} %refs_3_.1, s32[128,8]{1,0:T(8,128)} %copy.7.refs_4_, s32[128,8]{1,0:T(8,128)} %copy.8.refs_5_), custom_call_target="tpu_custom_call" | custom-call | flops 6000000000 | bytes 7000000 | tf_op jit(solution)/shard_map/pallas_call | solution.py:479
  124.7 3.0 %copy.10 = f32[32,16384]{1,0:T(8,128)} copy(f32[32,16384]{1,0:T(8,128)} %shard_map.64) | data formatting | bytes 4194304

commit v2 on v1

--- a/solution.py
+++ b/solution.py
@@ -42,7 +42,9 @@
 
 def dot3(a, b_high, b_low):
     high, low = split2(a)
-    return dot(high, b_high) + (dot(high, b_low) + dot(low, b_high))
+    n = a.shape[0]
+    both = dot(jnp.concatenate([high, low], axis=0), b_high)
+    return both[:n] + (dot(high, b_low) + both[n:])
 
 
 def from_square(d2):
@@ -108,23 +110,35 @@
     return SCALE * (jnp.where(left, half, -half) + jnp.where(left, r0, r1) * units[None])
 
 
+def couple_square(coefs, d2):
+    across = (lax.broadcasted_iota(jnp.int32, (128, 128), 0) < K) != lower_lanes((128, 128))
+    tile = jnp.where(across, from_square(d2), 0.0)
+    tile_high, tile_low = split2(tile)
+    return dot3(coefs, tile_high, tile_low)
+
+
+def block_diagonal(x):
+    leaf = lax.broadcasted_iota(jnp.int32, x.shape, 1) // PT
+    wide = x.astype(F32)
+    return jnp.concatenate(
+        [jnp.where(leaf == k, wide, 0.0) for k in range(GRP)], axis=0
+    ).astype(BF16)
+
+
 def couple_pair(coefs, coords):
     columns = jnp.transpose(coords)
     d2 = None
     for k in range(3):
         gap = columns[:, k : k + 1] - coords[k : k + 1, :]
         d2 = gap * gap if d2 is None else d2 + gap * gap
-    across = (lax.broadcasted_iota(jnp.int32, (128, 128), 0) < K) != lower_lanes((128, 128))
-    tile = jnp.where(across, from_square(d2), 0.0)
-    tile_high, tile_low = split2(tile)
-    return dot3(coefs, tile_high, tile_low)
+    return couple_square(coefs, d2)
 
 
 def kernel(
     nl, ns,
     charges, points, basis, transfer, near_list, coupling_list,
     out,
-    p8, xe, oe, ua, va, vb, weight,
+    p8, xe, oe, ua, va, vb, xd, inner0, cross0, inner1, cross1, weight,
     leaf_pts, centers, radii, pairs, pair_co, sib,
     up_pair, v_left, v_right, c_left, c_right, lc,
     send_coef, halo_coef, send_shape, halo_shape,
@@ -254,16 +268,18 @@
     ]
     got_sub[sub_id] = root[...]
 
-    @pl.loop(0, 21)
+    @pl.loop(0, 9)
     def _(i):
-        for s in range(3):
-            sib[i * 3 + s] = couple_pair(pairs[LD // 2 + i * 3 + s], pair_co[i * 3 + s])
+        for s in range(7):
+            u, v = features(pair_co[i * 7 + s], 0)
+            d2 = dot_tn(u.astype(BF16), v.astype(BF16))
+            sib[i * 7 + s] = couple_square(pairs[LD // 2 + i * 7 + s], d2)
 
     xe[:, GW : EXT - GW] = charges[...]
     oe[:, GW : EXT - GW] = charges[...].astype(F32)
     leaf_row = lax.broadcasted_iota(jnp.int32, (LD, 1), 0)
     base = first + (leaf_row // GRP) * GRP - GRP
-    listed = near_list[...]
+    listed = jnp.transpose(near_list[...])
     relative = jnp.where(listed >= 0, listed - base, -1)
     weight[...] = jnp.zeros_like(weight)
     for k in range(3 * GRP):
@@ -285,36 +301,62 @@
         ua[:, lanes] = u.astype(BF16)
         va[:, lanes] = v.astype(BF16)
         vb[:, lanes] = features(SCALE * low, 0)[1].astype(BF16)
+        xd[pl.ds(pl.multiple_of(g * 128, 128), 128), :] = block_diagonal(xe[:, lanes])
 
     oe[:, 0:GW] = jnp.zeros((R, GW), F32)
     oe[:, EXT - GW : EXT] = jnp.zeros((R, GW), F32)
 
-    @pl.loop(0, GROUPS + 1)
-    def _(g):
+    def near_tiles(g, inner, cross):
         here = pl.ds(pl.multiple_of(g * GW, GW), GW)
         there = pl.ds(pl.multiple_of(g * GW + GW, GW), GW)
-        u = ua[:, here]
-        v = jnp.concatenate([va[:, here], vb[:, there]], axis=1)
-        x = jnp.concatenate([xe[:, here], xe[:, there]], axis=1)
-        total = [oe[:, here][:, j * PT : (j + 1) * PT] for j in range(GRP)]
-        total += [oe[:, there][:, j * PT : (j + 1) * PT] for j in range(GRP)]
-
-        def times(target, source):
-            k = source + GRP if target < GRP else source
+        u, v, v_next = ua[:, here], va[:, here], vb[:, there]
+        for i in range(GRP):
+            rows = slice(i * PT, (i + 1) * PT)
+            inner[rows, i * PT :] = from_square(dot_tn(u[:, rows], v[:, i * PT :])).astype(BF16)
+            cross[rows, :] = from_square(dot_tn(u[:, rows], v_next)).astype(BF16)
+
+    def near_sums(g, inner, cross):
+        here = pl.ds(pl.multiple_of(g * GW, GW), GW)
+        there = pl.ds(pl.multiple_of(g * GW + GW, GW), GW)
+
+        def times(k, target):
             return weight[k, pl.ds(g * GRP + target, 1), :]
 
-        for i in range(GRP):
-            d2 = dot_tn(u[:, i * PT : (i + 1) * PT], v[:, i * PT :])
-            tile = from_square(d2).astype(BF16)
-            part = dot(x[:, i * PT : (i + 1) * PT], tile)
-            for j in range(i, 2 * GRP):
-                at = (j - i) * PT
-                total[j] = total[j] + times(j, i) * part[:, at : at + PT]
-                if j > i:
-                    back = dot_nt(x[:, j * PT : (j + 1) * PT], tile[:, at : at + PT])
-                    total[i] = total[i] + times(i, j) * back
-        oe[:, here] = jnp.concatenate(total[:GRP], axis=1)
-        oe[:, there] = jnp.concatenate(total[GRP:], axis=1)
+        def part(block, source, target=0):
+            return block[source * R : (source + 1) * R, target * PT : (target + 1) * PT]
+
+        x = xd[pl.ds(pl.multiple_of(g * 128, 128), 128), :]
+        x_next = xd[pl.ds(pl.multiple_of(g * 128 + 128, 128), 128), :]
+        own = [part(oe[:, here], 0, j) for j in range(GRP)]
+        following = [part(oe[:, there], 0, j) for j in range(GRP)]
+        for j in range(GRP):
+            n = j + 1
+            to_later = dot(x[: n * R, : n * PT], inner[: n * PT, j * PT : (j + 1) * PT])
+            for i in range(n):
+                own[j] = own[j] + times(GRP + i, j) * part(to_later, i)
+        for i in range(GRP - 1):
+            n = i + 1
+            to_earlier = dot_nt(x[n * R :, n * PT :], inner[i * PT : n * PT, n * PT :])
+            for j in range(n, GRP):
+                own[i] = own[i] + times(GRP + j, i) * part(to_earlier, j - n)
+        forth, back = dot(x, cross[...]), dot_nt(x_next, cross[...])
+        for j in range(GRP):
+            for i in range(GRP):
+                following[j] = following[j] + times(i, GRP + j) * part(forth, i, j)
+                own[i] = own[i] + times(2 * GRP + j, i) * part(back, j, i)
+        oe[:, here] = jnp.concatenate(own, axis=1)
+        oe[:, there] = jnp.concatenate(following, axis=1)
+
+    near_tiles(0, inner0, cross0)
+
+    @pl.loop(0, GROUPS // 2)
+    def _(h):
+        near_tiles(2 * h + 1, inner1, cross1)
+        near_sums(2 * h, inner0, cross0)
+        near_tiles(2 * h + 2, inner0, cross0)
+        near_sums(2 * h + 1, inner1, cross1)
+
+    near_sums(GROUPS, inner0, cross0)
 
     def climb(got, width, level0, index):
         coefs = got[:, 0:R, :]
@@ -394,8 +436,7 @@
     for ref in (c_left, c_right, v_left, v_right):
         ref[dead] = jnp.zeros(ref.shape[1:], BF16)
 
-    @pl.loop(0, LD // 2)
-    def _(m):
+    def listed(m):
         u = jnp.transpose(up_pair[m].astype(F32)).astype(BF16)
         tiles, sources = [], []
         for s in range(2):
@@ -404,7 +445,7 @@
             for t in range(4):
                 picked = []
                 for slot in (2 * t, 2 * t + 1):
-                    j = coupling_list[leaf, slot]
+                    j = coupling_list[slot, leaf]
                     near_by = jnp.clip(j - first + REACH, 0, dead - 1)
                     picked.append(jnp.where(j >= 0, near_by, dead))
                 vs.append(v_left[picked[0]] + v_right[picked[1]])
@@ -412,8 +453,14 @@
             d2 = dot(u[s * K : (s + 1) * K], jnp.concatenate(vs, axis=1))
             tiles.append(from_square(d2).astype(BF16))
             sources.append(jnp.concatenate(cs, axis=1))
-        product = dot_nt(jnp.concatenate(sources, axis=0), jnp.concatenate(tiles, axis=0))
-        lc[m] = jnp.where(lane_half, product[:R], product[R:])
+        return jnp.concatenate(sources, axis=0), jnp.concatenate(tiles, axis=0)
+
+    @pl.loop(0, LD // 8)
+    def _(b):
+        operands = [listed(b * 4 + s) for s in range(4)]
+        for s in range(4):
+            product = dot_nt(*operands[s])
+            lc[b * 4 + s] = jnp.where(lane_half, product[:R], product[R:])
 
     for copy in leaf_copies:
         copy.wait()
@@ -488,6 +535,11 @@
             pltpu.VMEM((FEAT, EXT), BF16),
             pltpu.VMEM((FEAT, EXT), BF16),
             pltpu.VMEM((FEAT, EXT), BF16),
+            pltpu.VMEM(((GROUPS + 2) * 128, GW), BF16),
+            pltpu.VMEM((GW, GW), BF16),
+            pltpu.VMEM((GW, GW), BF16),
+            pltpu.VMEM((GW, GW), BF16),
+            pltpu.VMEM((GW, GW), BF16),
             pltpu.VMEM((3 * GRP, LD + 2 * GRP, 128), F32),
             pltpu.VMEM((LD, 8, 128), F32),
             pltpu.VMEM((LD, 8, 128), F32),
@@ -521,7 +573,7 @@
         cost_estimate=pl.CostEstimate(
             flops=6 * 10**9, bytes_accessed=7 * 10**6, transcendentals=4 * 10**7
         ),
-    )(charges, points, basis, transfer, near_list, coupling_list)
+    )(charges, points, basis, transfer, near_list.T, coupling_list.T)
 
 
 def solution(mesh):

time: 128 us -> 83.2 us (0.65)
  Pallas kernels: 122 us -> 80 us
  local copies, waits for them, and re-layouts: 5.86 us -> 3.05 us
    pallas_call x1, Pallas kernels: 122 us -> 80 us  [per_device(): pl.pallas_call(body, out_shape=jax.ShapeDtypeStruct((R, LD * PT), F32), i...]
    unnamed x3 -> x1, local copies, waits for them, and re-layouts: 5.86 us -> 3.05 us
where the time goes in v2:
time: 83.2 us; the launch traced here: 83.1 us
  Pallas kernels  80 us (96%)
  local copies, waits for them, and re-layouts  3.05 us (4%)
    pallas_call x1, Pallas kernels, per_device(): pl.pallas_call(body, out_shape=jax.ShapeDtypeStruct((R, LD * PT), F32), i...  80 us
    unnamed x1, local copies, waits for them, and re-layouts  3.05 us

profile of v2, /device:TPU:0, one launch (start us, length us, event | category | flops | bytes accessed | tf_op | source)
XLA Modules:
  0.0 83.1 jit_solution(11411737680109349779)
XLA Ops:
  0.0 80.0 %shard_map.64 = f32[32,16384]{1,0:T(8,128)} custom-call(bf16[32,16384]{1,0:T(8,128)(2,1)} %refs_0_.1, f32[3,16384]{1,0:T(4,128)} %refs_1_.1, bf16[128,64,128]{2,1,0:T(8,128)(2,1)} %refs_2_.1, f32[2,64,64]{2,1,0:T(8,128)} %refs_3_.1, s32[8,128]{1,0:T(8,128)} %bitcast.2, s32[8,128]{1,0:T(8,128)} %bitcast.3), custom_call_target="tpu_custom_call" | custom-call | flops 6000000000 | bytes 7000000 | tf_op jit(solution)/shard_map/pallas_call | solution.py:526
  80.0 3.0 %copy.8 = f32[32,16384]{1,0:T(8,128)} copy(f32[32,16384]{1,0:T(8,128)} %shard_map.64) | data formatting | bytes 4194304

commit v3 on v2

--- a/solution.py
+++ b/solution.py
@@ -17,7 +17,7 @@
 GW = GRP * PT
 GROUPS = LD // GRP
 EXT = (GROUPS + 2) * GW
-FEAT = 48
+FEAT = 32
 SCALE = math.log2(math.e) / 2.0
 TINY = 1e-30
 MESH = pl.DeviceIdType.MESH
@@ -61,11 +61,15 @@
     n2 = (norm - n1).astype(BF16).astype(F32)
     n3 = norm - n1 - n2
     row = lax.broadcasted_iota(jnp.int32, coords.shape, axis)
-    norms = jnp.where(row == 0, n1, jnp.where(row == 1, n2, jnp.where(row == 2, n3, 0.0)))
-    ones = jnp.where(row < 3, 1.0, 0.0)
-    high2, low2 = -2.0 * high, -2.0 * low
-    u = jnp.concatenate([high, high, low, low, norms, ones], axis=axis)
-    v = jnp.concatenate([high2, low2, high2, low2, ones, norms], axis=axis)
+    ones = jnp.where((row >= 4) & (row < 7), 1.0, 0.0)
+    norms = jnp.where(row == 0, n1, jnp.where(row == 1, n2, jnp.where(row == 2, n3, ones)))
+    both = high + pltpu.roll(low, 4, axis)
+    twice = -2.0 * both
+    zero = jnp.zeros_like(both)
+    u = jnp.concatenate([both, both, norms, zero], axis=axis)
+    v = jnp.concatenate(
+        [twice, pltpu.roll(twice, 4, axis), pltpu.roll(norms, 4, axis), zero], axis=axis
+    )
     return u, v
 
 
@@ -117,6 +121,18 @@
     return dot3(coefs, tile_high, tile_low)
 
 
+def couple_near_pair(coefs, coords):
+    u, v = features(coords, 0)
+    lower = lower_lanes(v.shape)
+    v_two = jnp.concatenate([jnp.where(lower, v, 0.0), jnp.where(lower, 0.0, v)], axis=0)
+    columns = jnp.transpose(u)
+    u_two = jnp.concatenate([columns[K:], columns[:K]], axis=1)
+    tile_high, tile_low = split2(from_square(dot(u_two.astype(BF16), v_two.astype(BF16))))
+    swapped = pltpu.roll(coefs, K, 1)
+    both = dot3(jnp.concatenate([swapped[:, :K], coefs[:, :K]], axis=0), tile_high, tile_low)
+    return jnp.where(lower_lanes((R, 128)), both[:R], both[R:])
+
+
 def block_diagonal(x):
     leaf = lax.broadcasted_iota(jnp.int32, x.shape, 1) // PT
     wide = x.astype(F32)
@@ -139,11 +155,11 @@
     charges, points, basis, transfer, near_list, coupling_list,
     out,
     p8, xe, oe, ua, va, vb, xd, inner0, cross0, inner1, cross1, weight,
-    leaf_pts, centers, radii, pairs, pair_co, sib,
-    up_pair, v_left, v_right, c_left, c_right, lc,
+    centers, radii, pairs, pair_co, sib,
+    up_pair, v_all, c_all, lc,
     send_coef, halo_coef, send_shape, halo_shape,
-    root, got_sub, root_b, got_leaf, path_pair, path_co, e0,
-    near_send, near_recv, coup_send, coup_recv, sub_send, sub_recv, leaf_send, leaf_recv,
+    root, got_sub, root_b, got_leaf, path_pair, path_co, d1,
+    near_send, near_recv, coup_send, coup_recv, sub_send, sub_recv, leaf_send, leaf_recv, local_sem,
 ):
     leaf_id, sub_id = lax.axis_index("leaf"), lax.axis_index("sub")
     count = nl * ns
@@ -166,6 +182,10 @@
         copy.start()
         return copy
 
+    own_charges = pltpu.make_async_copy(
+        charges, xe.at[:, pl.ds(GW, LD * PT)], local_sem.at[0]
+    )
+    own_charges.start()
     first = me * LD
     units = unit_rows()
     lane_half = lower_lanes((R, 128))
@@ -185,13 +205,12 @@
                        near_send.at[3], near_recv.at[3], right_dev))
     near_copies = copies
 
-    for c in range(LD):
-        leaf_pts[c] = p8[:, GW + c * PT : GW + (c + 1) * PT]
-
     @pl.loop(0, LD // 16)
     def _(block):
+        start = pl.multiple_of(GW + block * (16 * PT), 16 * PT // 4)
+        wide = p8[:, pl.ds(start, 16 * PT)]
+        pts = jnp.stack([wide[:, c * PT : (c + 1) * PT] for c in range(16)])
         rows = pl.ds(block * 16, 16)
-        pts = leaf_pts[rows]
         center = jnp.mean(pts, axis=2, keepdims=True)
         off = pts - center
         far = jnp.max(jnp.sum(off * off, axis=1, keepdims=True), axis=2, keepdims=True)
@@ -201,10 +220,12 @@
     row8 = lax.broadcasted_iota(jnp.int32, (8, 128), 0)
     lane8 = lax.broadcasted_iota(jnp.int32, (8, 128), 1)
 
-    packed = jnp.zeros((8, 128), F32)
-    for c in range(LD):
-        packed = jnp.where(lane8 == c, jnp.where(row8 < 3, centers[c], radii[c]), packed)
-    send_shape[...] = packed
+    packed_cen, packed_rad = centers[0], radii[0]
+    for c in range(1, LD):
+        packed_cen = jnp.where(lane8 == c, centers[c], packed_cen)
+        packed_rad = jnp.where(lane8 == c, radii[c], packed_rad)
+    send_shape[0:8, :] = packed_cen
+    send_shape[8:16, :] = packed_rad
 
     @pl.loop(0, LD // 16)
     def _(block):
@@ -240,13 +261,23 @@
 
     level_cen, level_rad = centers[...], radii[...]
     offset, n = 0, LD // 2
-    block = pairs[pl.ds(0, n)]
+    block = None
     while n > 1:
-        block = side_by_side(lift(block))
         level_cen, level_rad = merge_shapes(level_cen, level_rad)
+        if n >= 32:
+
+            def lift_part(i, offset=offset, n=n):
+                eight = pairs[pl.ds(offset + i * 8, 8)]
+                pairs[pl.ds(offset + n + i * 4, 4)] = side_by_side(lift(eight))
+
+            pl.loop(0, n // 8)(lift_part)
+        else:
+            if block is None:
+                block = pairs[pl.ds(offset, n)]
+            block = side_by_side(lift(block))
+            pairs[pl.ds(offset + n, n // 2)] = block
         offset += n
         n //= 2
-        pairs[pl.ds(offset, n)] = block
         pair_co[pl.ds(offset - LD // 2, n)] = pair_coords(level_cen, level_rad, units)
     root_coef = lift(block)[0]
     root_cen, root_rad = merge_shapes(level_cen, level_rad)
@@ -268,32 +299,30 @@
     ]
     got_sub[sub_id] = root[...]
 
-    @pl.loop(0, 9)
-    def _(i):
-        for s in range(7):
-            u, v = features(pair_co[i * 7 + s], 0)
-            d2 = dot_tn(u.astype(BF16), v.astype(BF16))
-            sib[i * 7 + s] = couple_square(pairs[LD // 2 + i * 7 + s], d2)
-
-    xe[:, GW : EXT - GW] = charges[...]
-    oe[:, GW : EXT - GW] = charges[...].astype(F32)
-    leaf_row = lax.broadcasted_iota(jnp.int32, (LD, 1), 0)
-    base = first + (leaf_row // GRP) * GRP - GRP
-    listed = jnp.transpose(near_list[...])
-    relative = jnp.where(listed >= 0, listed - base, -1)
-    weight[...] = jnp.zeros_like(weight)
+    leaf_lane = lax.broadcasted_iota(jnp.int32, (8, LD), 1)
+    base = first + (leaf_lane // GRP) * GRP - GRP
+    listed_leaf = near_list[...]
+    relative = jnp.where(listed_leaf >= 0, listed_leaf - base, -1)
+    slot_row = lax.broadcasted_iota(jnp.int32, (16, LD), 0)
+    counts = jnp.zeros((16, LD), F32)
     for k in range(3 * GRP):
-        times = jnp.sum(jnp.where(relative == k, 1.0, 0.0), axis=1, keepdims=True)
-        weight[k, GRP : GRP + LD, :] = jnp.broadcast_to(times, (LD, 128))
-
+        times = jnp.sum(jnp.where(relative == k, 1.0, 0.0), axis=0, keepdims=True)
+        counts = jnp.where(slot_row == k, times, counts)
+    columns = jnp.transpose(counts).astype(BF16)
+    for k in range(3 * GRP):
+        ones = jnp.where(slot_row == k, 1.0, 0.0).astype(BF16)
+        weight[k, 0:8, :] = jnp.zeros((8, 128), F32)
+        weight[k, 8 : 8 + LD, :] = dot(columns, ones)
+        weight[k, 8 + LD : 16 + LD, :] = jnp.zeros((8, 128), F32)
+
+    own_charges.wait()
     for copy in near_copies:
         copy.wait()
 
-    @pl.loop(0, GROUPS + 2)
-    def _(g):
+    def near_features(g):
         lanes = pl.ds(pl.multiple_of(g * GW, GW), GW)
         row = lax.broadcasted_iota(jnp.int32, (8, GW), 0)
-        z0 = (me * GROUPS + g - 1).astype(F32)
+        z0 = lax.convert_element_type(me * GROUPS + g - 1, F32)
         corner = jnp.where(row == 2, z0, jnp.where(row < 2, 1.0, 0.0))
         low = p8[:, lanes] - corner
         shift = jnp.where(row == 2, 1.0, 0.0)
@@ -304,7 +333,6 @@
         xd[pl.ds(pl.multiple_of(g * 128, 128), 128), :] = block_diagonal(xe[:, lanes])
 
     oe[:, 0:GW] = jnp.zeros((R, GW), F32)
-    oe[:, EXT - GW : EXT] = jnp.zeros((R, GW), F32)
 
     def near_tiles(g, inner, cross):
         here = pl.ds(pl.multiple_of(g * GW, GW), GW)
@@ -320,7 +348,7 @@
         there = pl.ds(pl.multiple_of(g * GW + GW, GW), GW)
 
         def times(k, target):
-            return weight[k, pl.ds(g * GRP + target, 1), :]
+            return weight[k, pl.ds(g * GRP + target + GRP, 1), :]
 
         def part(block, source, target=0):
             return block[source * R : (source + 1) * R, target * PT : (target + 1) * PT]
@@ -328,7 +356,8 @@
         x = xd[pl.ds(pl.multiple_of(g * 128, 128), 128), :]
         x_next = xd[pl.ds(pl.multiple_of(g * 128 + 128, 128), 128), :]
         own = [part(oe[:, here], 0, j) for j in range(GRP)]
-        following = [part(oe[:, there], 0, j) for j in range(GRP)]
+        nugget = xe[:, there].astype(F32)
+        following = [part(nugget, 0, j) for j in range(GRP)]
         for j in range(GRP):
             n = j + 1
             to_later = dot(x[: n * R, : n * PT], inner[: n * PT, j * PT : (j + 1) * PT])
@@ -347,6 +376,47 @@
         oe[:, here] = jnp.concatenate(own, axis=1)
         oe[:, there] = jnp.concatenate(following, axis=1)
 
+    for copy in coup_copies:
+        copy.wait()
+    middle_row = lax.broadcasted_iota(jnp.int32, (1, 8, 128), 1)
+    middle = jnp.where(
+        middle_row == 2,
+        (me * GROUPS + GROUPS // 2).astype(F32),
+        jnp.where(middle_row < 2, 1.0, 0.0),
+    )
+
+    def put_leaves(where, cen, rad):
+        u, v = features(SCALE * (cen - middle + rad * units[None]), 1)
+        v_all[pl.ds(where, 8)] = v.astype(BF16)
+        return u
+
+    def put_coefs(where, two):
+        other = pltpu.roll(two, K, 1)
+        c_all[where] = jnp.where(lane_half, two, other).astype(BF16)
+        c_all[where + 1] = jnp.where(lane_half, other, two).astype(BF16)
+
+    def coupling_side(b):
+        u = put_leaves(REACH + b * 8, centers[pl.ds(b * 8, 8)], radii[pl.ds(b * 8, 8)])
+        up_pair[pl.ds(b * 4, 4)] = side_by_side(u).astype(BF16)
+        for s in range(4):
+            put_coefs(REACH + b * 8 + 2 * s, pairs[b * 4 + s])
+        side, eighth = b // 8, lax.rem(b, 8)
+        start = side * (REACH + LD) + eighth * 8
+        turn = lax.rem(LD + side * REACH + REACH - eighth * 8, LD)
+        shape = pltpu.roll(halo_shape[side], turn, 1)
+        cens = [jnp.broadcast_to(shape[0:8, s : s + 1], (8, 128)) for s in range(8)]
+        rads = [jnp.broadcast_to(shape[8:16, s : s + 1], (8, 128)) for s in range(8)]
+        put_leaves(start, jnp.stack(cens), jnp.stack(rads))
+        for s in range(4):
+            put_coefs(start + 2 * s, halo_coef[side, eighth * 4 + s].astype(F32))
+
+    def siblings(b):
+        for s in range(4):
+            i = jnp.minimum(b * 4 + s, LD // 2 - 2)
+            sib[i] = couple_near_pair(pairs[LD // 2 + i], pair_co[i])
+
+    for g in range(4):
+        near_features(g)
     near_tiles(0, inner0, cross0)
 
     @pl.loop(0, GROUPS // 2)
@@ -355,6 +425,10 @@
         near_sums(2 * h, inner0, cross0)
         near_tiles(2 * h + 2, inner0, cross0)
         near_sums(2 * h + 1, inner1, cross1)
+        for s in range(2):
+            near_features(jnp.minimum(2 * h + 4 + s, GROUPS + 1))
+        coupling_side(h)
+        siblings(h)
 
     near_sums(GROUPS, inner0, cross0)
 
@@ -384,57 +458,10 @@
     ]
     got_leaf[leaf_id] = root_b[...]
 
-    for copy in coup_copies:
-        copy.wait()
-    middle_row = lax.broadcasted_iota(jnp.int32, (1, 8, 128), 1)
-    middle = jnp.where(
-        middle_row == 2,
-        (me * GROUPS + GROUPS // 2).astype(F32),
-        jnp.where(middle_row < 2, 1.0, 0.0),
-    )
-
-    def put_leaves(where, cen, rad):
-        u, v = features(SCALE * (cen - middle + rad * units[None]), 1)
-        lower = lower_lanes(v.shape)
-        v_left[pl.ds(where, 8)] = jnp.where(lower, v, 0.0).astype(BF16)
-        v_right[pl.ds(where, 8)] = jnp.where(lower, 0.0, v).astype(BF16)
-        return u
-
-    def put_coefs(where, two):
-        lower = lower_lanes((R, 128))
-        first_left = jnp.where(lower, two, 0.0)
-        second_right = jnp.where(lower, 0.0, two)
-        c_left[where] = first_left.astype(BF16)
-        c_right[where] = pltpu.roll(first_left, K, 1).astype(BF16)
-        c_left[where + 1] = pltpu.roll(second_right, K, 1).astype(BF16)
-        c_right[where + 1] = second_right.astype(BF16)
-
-    @pl.loop(0, LD // 8)
-    def _(b):
-        u = put_leaves(REACH + b * 8, centers[pl.ds(b * 8, 8)], radii[pl.ds(b * 8, 8)])
-        up_pair[pl.ds(b * 4, 4)] = side_by_side(u).astype(BF16)
-        for s in range(4):
-            put_coefs(REACH + b * 8 + 2 * s, pairs[b * 4 + s])
-
-    for side, start, lane0 in ((0, 0, REACH), (1, REACH + LD, 0)):
-        shape = halo_shape[side]
-        for b in range(REACH // 8):
-            cens, rads = [], []
-            for s in range(8):
-                lane = lane0 + b * 8 + s
-                column = jnp.broadcast_to(shape[:, lane : lane + 1], (8, 128))
-                cens.append(jnp.where(row8 < 3, column, 0.0))
-                rads.append(jnp.broadcast_to(column[3:4, :], (8, 128)))
-            put_leaves(start + b * 8, jnp.stack(cens), jnp.stack(rads))
-
-        @pl.loop(0, REACH // 16)
-        def _(b):
-            for s in range(8):
-                put_coefs(start + b * 16 + 2 * s, halo_coef[side, b * 8 + s].astype(F32))
-
     dead = LD + 2 * REACH
-    for ref in (c_left, c_right, v_left, v_right):
+    for ref in (c_all, v_all):
         ref[dead] = jnp.zeros(ref.shape[1:], BF16)
+    first_half = lower_lanes((FEAT, 128))
 
     def listed(m):
         u = jnp.transpose(up_pair[m].astype(F32)).astype(BF16)
@@ -448,8 +475,8 @@
                     j = coupling_list[slot, leaf]
                     near_by = jnp.clip(j - first + REACH, 0, dead - 1)
                     picked.append(jnp.where(j >= 0, near_by, dead))
-                vs.append(v_left[picked[0]] + v_right[picked[1]])
-                cs.append(c_left[picked[0]] + c_right[picked[1]])
+                vs.append(jnp.where(first_half, v_all[picked[0]], v_all[picked[1]]))
+                cs.append(jnp.where(first_half, c_all[picked[0]], c_all[picked[1]]))
             d2 = dot(u[s * K : (s + 1) * K], jnp.concatenate(vs, axis=1))
             tiles.append(from_square(d2).astype(BF16))
             sources.append(jnp.concatenate(cs, axis=1))
@@ -496,13 +523,14 @@
         n *= 2
         offset -= n
         block = block + sib[pl.ds(offset, n)]
-    e0[...] = spread(block)
+    d1[...] = block
 
     @pl.loop(0, LD // 16)
     def _(b):
+        below = spread(d1[pl.ds(b * 4, 4)])
         for s in range(8):
             m = b * 8 + s
-            coef = lc[m] + e0[m]
+            coef = lc[m] + below[s]
             stacked = jnp.concatenate(
                 [jnp.where(lane_half, coef, 0.0), jnp.where(lane_half, 0.0, coef)], axis=0
             ).astype(BF16)
@@ -540,8 +568,7 @@
             pltpu.VMEM((GW, GW), BF16),
             pltpu.VMEM((GW, GW), BF16),
             pltpu.VMEM((GW, GW), BF16),
-            pltpu.VMEM((3 * GRP, LD + 2 * GRP, 128), F32),
-            pltpu.VMEM((LD, 8, 128), F32),
+            pltpu.VMEM((3 * GRP, LD + 16, 128), F32),
             pltpu.VMEM((LD, 8, 128), F32),
             pltpu.VMEM((LD, 8, 128), F32),
             pltpu.VMEM((LD, R, 128), F32),
@@ -549,23 +576,21 @@
             pltpu.VMEM((LD // 2, R, 128), F32),
             pltpu.VMEM((LD // 2, FEAT, 128), BF16),
             pltpu.VMEM((total, FEAT, 128), BF16),
-            pltpu.VMEM((total, FEAT, 128), BF16),
-            pltpu.VMEM((total, R, 128), BF16),
             pltpu.VMEM((total, R, 128), BF16),
             pltpu.VMEM((LD // 2, R, 128), F32),
             pltpu.VMEM((LD // 2, R, 128), BF16),
             pltpu.VMEM((2, REACH // 2, R, 128), BF16),
-            pltpu.VMEM((8, 128), F32),
-            pltpu.VMEM((2, 8, 128), F32),
+            pltpu.VMEM((16, 128), F32),
+            pltpu.VMEM((2, 16, 128), F32),
             pltpu.VMEM((R + 8, 128), F32),
             pltpu.VMEM((ns, R + 8, 128), F32),
             pltpu.VMEM((R + 8, 128), F32),
             pltpu.VMEM((nl, R + 8, 128), F32),
             pltpu.VMEM((levels, widest, R, 128), F32),
             pltpu.VMEM((levels, widest, 8, 128), F32),
-            pltpu.VMEM((LD // 2, R, 128), F32),
+            pltpu.VMEM((LD // 4, R, 128), F32),
             dma((4,)), dma((4,)), dma((4,)), dma((4,)),
-            dma((ns,)), dma((ns,)), dma((nl,)), dma((nl,)),
+            dma((ns,)), dma((ns,)), dma((nl,)), dma((nl,)), dma((1,)),
         ],
         compiler_params=pltpu.CompilerParams(
             collective_id=0, has_side_effects=True, vmem_limit_bytes=56 * 2**20

time: 83.2 us -> 78.4 us (0.942)
  Pallas kernels: 80 us -> 75.2 us
    pallas_call x1, Pallas kernels: 80 us -> 75.2 us  [per_device(): pl.pallas_call(body, out_shape=jax.ShapeDtypeStruct((R, LD * PT), F32), i...]
where the time goes in v3:
time: 78.4 us; the launch traced here: 78.3 us
  Pallas kernels  75.2 us (96%)
  local copies, waits for them, and re-layouts  3.05 us (4%)
    pallas_call x1, Pallas kernels, per_device(): pl.pallas_call(body, out_shape=jax.ShapeDtypeStruct((R, LD * PT), F32), i...  75.2 us
    unnamed x1, local copies, waits for them, and re-layouts  3.05 us

profile of v3, /device:TPU:0, one launch (start us, length us, event | category | flops | bytes accessed | tf_op | source)
XLA Modules:
  0.0 78.3 jit_solution(13381502785412749511)
XLA Ops:
  0.0 75.2 %shard_map.64 = f32[32,16384]{1,0:T(8,128)} custom-call(bf16[32,16384]{1,0:T(8,128)(2,1)} %refs_0_.1, f32[3,16384]{1,0:T(4,128)} %refs_1_.1, bf16[128,64,128]{2,1,0:T(8,128)(2,1)} %refs_2_.1, f32[2,64,64]{2,1,0:T(8,128)} %refs_3_.1, s32[8,128]{1,0:T(8,128)} %bitcast.2, s32[8,128]{1,0:T(8,128)} %bitcast.3), custom_call_target="tpu_custom_call" | custom-call | flops 6000000000 | bytes 7000000 | tf_op jit(solution)/shard_map/pallas_call | solution.py:554
  75.3 3.0 %copy.8 = f32[32,16384]{1,0:T(8,128)} copy(f32[32,16384]{1,0:T(8,128)} %shard_map.64) | data formatting | bytes 4194304

commit v4 on v3

--- a/solution.py
+++ b/solution.py
@@ -114,14 +114,7 @@
     return SCALE * (jnp.where(left, half, -half) + jnp.where(left, r0, r1) * units[None])
 
 
-def couple_square(coefs, d2):
-    across = (lax.broadcasted_iota(jnp.int32, (128, 128), 0) < K) != lower_lanes((128, 128))
-    tile = jnp.where(across, from_square(d2), 0.0)
-    tile_high, tile_low = split2(tile)
-    return dot3(coefs, tile_high, tile_low)
-
-
-def couple_near_pair(coefs, coords):
+def couple_pair(coefs, coords):
     u, v = features(coords, 0)
     lower = lower_lanes(v.shape)
     v_two = jnp.concatenate([jnp.where(lower, v, 0.0), jnp.where(lower, 0.0, v)], axis=0)
@@ -141,25 +134,16 @@
     ).astype(BF16)
 
 
-def couple_pair(coefs, coords):
-    columns = jnp.transpose(coords)
-    d2 = None
-    for k in range(3):
-        gap = columns[:, k : k + 1] - coords[k : k + 1, :]
-        d2 = gap * gap if d2 is None else d2 + gap * gap
-    return couple_square(coefs, d2)
-
-
 def kernel(
     nl, ns,
-    charges, points, basis, transfer, near_list, coupling_list,
-    out,
-    p8, xe, oe, ua, va, vb, xd, inner0, cross0, inner1, cross1, weight,
+    charges, points, basis_hbm, transfer, near_list, coupling_list,
+    out_hbm,
+    basis, out, p8, xe, oe, ua, va, vb, xd, inner0, cross0, inner1, cross1, weight,
     centers, radii, pairs, pair_co, sib,
     up_pair, v_all, c_all, lc,
     send_coef, halo_coef, send_shape, halo_shape,
     root, got_sub, root_b, got_leaf, path_pair, path_co, d1,
-    near_send, near_recv, coup_send, coup_recv, sub_send, sub_recv, leaf_send, leaf_recv, local_sem,
+    near_send, near_recv, coup_send, coup_recv, sub_send, sub_recv, leaf_send, leaf_recv, local_sem, out_sem,
 ):
     leaf_id, sub_id = lax.axis_index("leaf"), lax.axis_index("sub")
     count = nl * ns
@@ -186,6 +170,8 @@
         charges, xe.at[:, pl.ds(GW, LD * PT)], local_sem.at[0]
     )
     own_charges.start()
+    own_basis = pltpu.make_async_copy(basis_hbm, basis, local_sem.at[1])
+    own_basis.start()
     first = me * LD
     units = unit_rows()
     lane_half = lower_lanes((R, 128))
@@ -193,11 +179,12 @@
     p8[3:8, GW : EXT - GW] = jnp.zeros((5, LD * PT), F32)
     p8[0:3, GW : EXT - GW] = points[...]
 
+    own_charges.wait()
     pl.semaphore_wait(barrier, len(partners))
     copies = []
-    copies.append(send(charges.at[:, pl.ds(0, GW)], xe.at[:, pl.ds(EXT - GW, GW)],
+    copies.append(send(xe.at[:, pl.ds(GW, GW)], xe.at[:, pl.ds(EXT - GW, GW)],
                        near_send.at[0], near_recv.at[0], left_dev))
-    copies.append(send(charges.at[:, pl.ds(LD * PT - GW, GW)], xe.at[:, pl.ds(0, GW)],
+    copies.append(send(xe.at[:, pl.ds(EXT - 2 * GW, GW)], xe.at[:, pl.ds(0, GW)],
                        near_send.at[1], near_recv.at[1], right_dev))
     copies.append(send(p8.at[:, pl.ds(GW, GW)], p8.at[:, pl.ds(EXT - GW, GW)],
                        near_send.at[2], near_recv.at[2], left_dev))
@@ -205,12 +192,12 @@
                        near_send.at[3], near_recv.at[3], right_dev))
     near_copies = copies
 
-    @pl.loop(0, LD // 16)
+    @pl.loop(0, LD // 32)
     def _(block):
-        start = pl.multiple_of(GW + block * (16 * PT), 16 * PT // 4)
-        wide = p8[:, pl.ds(start, 16 * PT)]
-        pts = jnp.stack([wide[:, c * PT : (c + 1) * PT] for c in range(16)])
-        rows = pl.ds(block * 16, 16)
+        start = pl.multiple_of(GW + block * (32 * PT), GW)
+        wide = p8[:, pl.ds(start, 32 * PT)]
+        pts = jnp.stack([wide[:, c * PT : (c + 1) * PT] for c in range(32)])
+        rows = pl.ds(block * 32, 32)
         center = jnp.mean(pts, axis=2, keepdims=True)
         off = pts - center
         far = jnp.max(jnp.sum(off * off, axis=1, keepdims=True), axis=2, keepdims=True)
@@ -227,11 +214,13 @@
     send_shape[0:8, :] = packed_cen
     send_shape[8:16, :] = packed_rad
 
-    @pl.loop(0, LD // 16)
+    own_basis.wait()
+
+    @pl.loop(0, LD // 32)
     def _(block):
-        for s in range(8):
-            m = block * 8 + s
-            x = charges[:, pl.ds(pl.multiple_of(m * 256, 256), 256)]
+        for s in range(16):
+            m = block * 16 + s
+            x = xe[:, pl.ds(pl.multiple_of(GW + m * 256, 256), 256)]
             stacked = jnp.concatenate([x[:, :128], x[:, 128:]], axis=0)
             both = basis[pl.ds(2 * m, 2)].reshape(2 * K, PT)
             product = dot_nt(stacked, both)
@@ -315,7 +304,6 @@
         weight[k, 8 : 8 + LD, :] = dot(columns, ones)
         weight[k, 8 + LD : 16 + LD, :] = jnp.zeros((8, 128), F32)
 
-    own_charges.wait()
     for copy in near_copies:
         copy.wait()
 
@@ -376,8 +364,6 @@
         oe[:, here] = jnp.concatenate(own, axis=1)
         oe[:, there] = jnp.concatenate(following, axis=1)
 
-    for copy in coup_copies:
-        copy.wait()
     middle_row = lax.broadcasted_iota(jnp.int32, (1, 8, 128), 1)
     middle = jnp.where(
         middle_row == 2,
@@ -395,40 +381,54 @@
         c_all[where] = jnp.where(lane_half, two, other).astype(BF16)
         c_all[where + 1] = jnp.where(lane_half, other, two).astype(BF16)
 
-    def coupling_side(b):
+    def coupling_own(b):
         u = put_leaves(REACH + b * 8, centers[pl.ds(b * 8, 8)], radii[pl.ds(b * 8, 8)])
         up_pair[pl.ds(b * 4, 4)] = side_by_side(u).astype(BF16)
         for s in range(4):
             put_coefs(REACH + b * 8 + 2 * s, pairs[b * 4 + s])
-        side, eighth = b // 8, lax.rem(b, 8)
-        start = side * (REACH + LD) + eighth * 8
-        turn = lax.rem(LD + side * REACH + REACH - eighth * 8, LD)
+
+    def coupling_halo(side, b):
+        start = side * (REACH + LD) + b * 8
+        turn = lax.rem(LD + (1 - side) * REACH - b * 8, LD)
         shape = pltpu.roll(halo_shape[side], turn, 1)
         cens = [jnp.broadcast_to(shape[0:8, s : s + 1], (8, 128)) for s in range(8)]
         rads = [jnp.broadcast_to(shape[8:16, s : s + 1], (8, 128)) for s in range(8)]
         put_leaves(start, jnp.stack(cens), jnp.stack(rads))
         for s in range(4):
-            put_coefs(start + 2 * s, halo_coef[side, eighth * 4 + s].astype(F32))
+            put_coefs(start + 2 * s, halo_coef[side, b * 4 + s].astype(F32))
 
     def siblings(b):
         for s in range(4):
             i = jnp.minimum(b * 4 + s, LD // 2 - 2)
-            sib[i] = couple_near_pair(pairs[LD // 2 + i], pair_co[i])
+            sib[i] = couple_pair(pairs[LD // 2 + i], pair_co[i])
 
     for g in range(4):
         near_features(g)
     near_tiles(0, inner0, cross0)
 
-    @pl.loop(0, GROUPS // 2)
-    def _(h):
+    def near_turn(h):
         near_tiles(2 * h + 1, inner1, cross1)
         near_sums(2 * h, inner0, cross0)
         near_tiles(2 * h + 2, inner0, cross0)
         near_sums(2 * h + 1, inner1, cross1)
         for s in range(2):
             near_features(jnp.minimum(2 * h + 4 + s, GROUPS + 1))
-        coupling_side(h)
         siblings(h)
+
+    @pl.loop(0, GROUPS // 4)
+    def _(h):
+        near_turn(h)
+        coupling_own(2 * h)
+        coupling_own(2 * h + 1)
+
+    for copy in coup_copies:
+        copy.wait()
+
+    @pl.loop(0, GROUPS // 4)
+    def _(h):
+        near_turn(GROUPS // 4 + h)
+        coupling_halo(0, h)
+        coupling_halo(1, h)
 
     near_sums(GROUPS, inner0, cross0)
 
@@ -482,12 +482,14 @@
             sources.append(jnp.concatenate(cs, axis=1))
         return jnp.concatenate(sources, axis=0), jnp.concatenate(tiles, axis=0)
 
-    @pl.loop(0, LD // 8)
-    def _(b):
+    def couple_four(b):
         operands = [listed(b * 4 + s) for s in range(4)]
         for s in range(4):
             product = dot_nt(*operands[s])
             lc[b * 4 + s] = jnp.where(lane_half, product[:R], product[R:])
+
+    beside = 2
+    pl.loop(0, LD // 8 - beside)(couple_four)
 
     for copy in leaf_copies:
         copy.wait()
@@ -524,12 +526,18 @@
         offset -= n
         block = block + sib[pl.ds(offset, n)]
     d1[...] = block
-
-    @pl.loop(0, LD // 16)
+    for b in range(LD // 8 - beside, LD // 8):
+        couple_four(b)
+
+    def put_out(b):
+        lanes = pl.ds(pl.multiple_of(b * 32 * PT, 32 * PT), 32 * PT)
+        return pltpu.make_async_copy(out.at[:, lanes], out_hbm.at[:, lanes], out_sem.at[b])
+
+    @pl.loop(0, LD // 32)
     def _(b):
-        below = spread(d1[pl.ds(b * 4, 4)])
-        for s in range(8):
-            m = b * 8 + s
+        below = spread(d1[pl.ds(b * 8, 8)])
+        for s in range(16):
+            m = b * 16 + s
             coef = lc[m] + below[s]
             stacked = jnp.concatenate(
                 [jnp.where(lane_half, coef, 0.0), jnp.where(lane_half, 0.0, coef)], axis=0
@@ -538,6 +546,10 @@
             start = pl.multiple_of(m * 256, 256)
             near = oe[:, pl.ds(pl.multiple_of(GW + m * 256, 256), 256)]
             out[:, pl.ds(start, 256)] = near + jnp.concatenate([far[:R], far[R:]], axis=1)
+        put_out(b).start()
+
+    for b in range(LD // 32):
+        put_out(b).wait()
 
 
 def per_device(charges, points, basis, transfer, near_list, coupling_list):
@@ -545,6 +557,7 @@
     levels = (nl * ns).bit_length() - 1
     widest = max(nl, ns) // 2
     vmem = pl.BlockSpec(memory_space=pltpu.VMEM)
+    hbm = pl.BlockSpec(memory_space=pl.ANY)
     total = LD + 2 * REACH + 1
 
     def body(*refs):
@@ -554,9 +567,11 @@
     return pl.pallas_call(
         body,
         out_shape=jax.ShapeDtypeStruct((R, LD * PT), F32),
-        in_specs=[vmem] * 5 + [pl.BlockSpec(memory_space=pltpu.SMEM)],
-        out_specs=vmem,
+        in_specs=[hbm, vmem, hbm, vmem, vmem, pl.BlockSpec(memory_space=pltpu.SMEM)],
+        out_specs=hbm,
         scratch_shapes=[
+            pltpu.VMEM((LD, K, PT), BF16),
+            pltpu.VMEM((R, LD * PT), F32),
             pltpu.VMEM((8, EXT), F32),
             pltpu.VMEM((R, EXT), BF16),
             pltpu.VMEM((R, EXT), F32),
@@ -590,7 +605,7 @@
             pltpu.VMEM((levels, widest, 8, 128), F32),
             pltpu.VMEM((LD // 4, R, 128), F32),
             dma((4,)), dma((4,)), dma((4,)), dma((4,)),
-            dma((ns,)), dma((ns,)), dma((nl,)), dma((nl,)), dma((1,)),
+            dma((ns,)), dma((ns,)), dma((nl,)), dma((nl,)), dma((2,)), dma((LD // 32,)),
         ],
         compiler_params=pltpu.CompilerParams(
             collective_id=0, has_side_effects=True, vmem_limit_bytes=56 * 2**20

time: 78.4 us -> 72.6 us (0.926)
  Pallas kernels: 75.2 us -> 69.4 us
    pallas_call x1, Pallas kernels: 75.2 us -> 69.4 us  [per_device(): pl.pallas_call(body, out_shape=jax.ShapeDtypeStruct((R, LD * PT), F32), i...]
where the time goes in v4:
time: 72.6 us; the launch traced here: 72.5 us
  Pallas kernels  69.4 us (96%)
  local copies, waits for them, and re-layouts  3.05 us (4%)
    pallas_call x1, Pallas kernels, per_device(): pl.pallas_call(body, out_shape=jax.ShapeDtypeStruct((R, LD * PT), F32), i...  69.4 us
    unnamed x1, local copies, waits for them, and re-layouts  3.05 us

profile of v4, /device:TPU:0, one launch (start us, length us, event | category | flops | bytes accessed | tf_op | source)
XLA Modules:
  0.0 72.5 jit_solution(3088844599706291407)
XLA Ops:
  0.0 69.4 %shard_map.64 = f32[32,16384]{1,0:T(8,128)} custom-call(bf16[32,16384]{1,0:T(8,128)(2,1)} %refs_0_.1, f32[3,16384]{1,0:T(4,128)} %refs_1_.1, bf16[128,64,128]{2,1,0:T(8,128)(2,1)} %refs_2_.1, f32[2,64,64]{2,1,0:T(8,128)} %refs_3_.1, s32[8,128]{1,0:T(8,128)} %bitcast.2, s32[8,128]{1,0:T(8,128)} %bitcast.3), custom_call_target="tpu_custom_call" | custom-call | flops 6000000000 | bytes 7000000 | tf_op jit(solution)/shard_map/pallas_call | solution.py:567
  69.4 3.0 %copy.8 = f32[32,16384]{1,0:T(8,128)} copy(f32[32,16384]{1,0:T(8,128)} %shard_map.64) | data formatting | bytes 4194304

commit v5 on v4

--- a/solution.py
+++ b/solution.py
@@ -256,10 +256,10 @@
         if n >= 32:
 
             def lift_part(i, offset=offset, n=n):
-                eight = pairs[pl.ds(offset + i * 8, 8)]
-                pairs[pl.ds(offset + n + i * 4, 4)] = side_by_side(lift(eight))
-
-            pl.loop(0, n // 8)(lift_part)
+                some = pairs[pl.ds(offset + i * 16, 16)]
+                pairs[pl.ds(offset + n + i * 8, 8)] = side_by_side(lift(some))
+
+            pl.loop(0, n // 16)(lift_part)
         else:
             if block is None:
                 block = pairs[pl.ds(offset, n)]
@@ -346,11 +346,12 @@
         own = [part(oe[:, here], 0, j) for j in range(GRP)]
         nugget = xe[:, there].astype(F32)
         following = [part(nugget, 0, j) for j in range(GRP)]
-        for j in range(GRP):
-            n = j + 1
-            to_later = dot(x[: n * R, : n * PT], inner[: n * PT, j * PT : (j + 1) * PT])
-            for i in range(n):
-                own[j] = own[j] + times(GRP + i, j) * part(to_later, i)
+        for c in range(0, GRP, 2):
+            n = c + 2
+            to_later = dot(x[: n * R, : n * PT], inner[: n * PT, c * PT : n * PT])
+            for j in range(c, n):
+                for i in range(j + 1):
+                    own[j] = own[j] + times(GRP + i, j) * part(to_later, i, j - c)
         for i in range(GRP - 1):
             n = i + 1
             to_earlier = dot_nt(x[n * R :, n * PT :], inner[i * PT : n * PT, n * PT :])
@@ -404,6 +405,9 @@
 
     for g in range(4):
         near_features(g)
+    for inner in (inner0, inner1):
+        for c in (0, 2):
+            inner[(c + 1) * PT : (c + 2) * PT, c * PT : (c + 1) * PT] = jnp.zeros((PT, PT), BF16)
     near_tiles(0, inner0, cross0)
 
     def near_turn(h):
@@ -488,7 +492,7 @@
             product = dot_nt(*operands[s])
             lc[b * 4 + s] = jnp.where(lane_half, product[:R], product[R:])
 
-    beside = 2
+    beside = 4
     pl.loop(0, LD // 8 - beside)(couple_four)
 
     for copy in leaf_copies:

time: 72.6 us -> 70.8 us (0.975)
  Pallas kernels: 69.4 us -> 67.6 us
    pallas_call x1, Pallas kernels: 69.4 us -> 67.6 us  [per_device(): pl.pallas_call(body, out_shape=jax.ShapeDtypeStruct((R, LD * PT), F32), i...]
where the time goes in v5:
time: 70.8 us; the launch traced here: 70.7 us
  Pallas kernels  67.6 us (95%)
  local copies, waits for them, and re-layouts  3.05 us (4%)
    pallas_call x1, Pallas kernels, per_device(): pl.pallas_call(body, out_shape=jax.ShapeDtypeStruct((R, LD * PT), F32), i...  67.6 us
    unnamed x1, local copies, waits for them, and re-layouts  3.05 us

profile of v5, /device:TPU:0, one launch (start us, length us, event | category | flops | bytes accessed | tf_op | source)
XLA Modules:
  0.0 70.7 jit_solution(9442043751008647880)
XLA Ops:
  0.0 67.6 %shard_map.64 = f32[32,16384]{1,0:T(8,128)} custom-call(bf16[32,16384]{1,0:T(8,128)(2,1)} %refs_0_.1, f32[3,16384]{1,0:T(4,128)} %refs_1_.1, bf16[128,64,128]{2,1,0:T(8,128)(2,1)} %refs_2_.1, f32[2,64,64]{2,1,0:T(8,128)} %refs_3_.1, s32[8,128]{1,0:T(8,128)} %bitcast.2, s32[8,128]{1,0:T(8,128)} %bitcast.3), custom_call_target="tpu_custom_call" | custom-call | flops 6000000000 | bytes 7000000 | tf_op jit(solution)/shard_map/pallas_call | solution.py:571
  67.7 3.0 %copy.8 = f32[32,16384]{1,0:T(8,128)} copy(f32[32,16384]{1,0:T(8,128)} %shard_map.64) | data formatting | bytes 4194304

commit v6 on v5

--- a/solution.py
+++ b/solution.py
@@ -436,32 +436,6 @@
 
     near_sums(GROUPS, inner0, cross0)
 
-    def climb(got, width, level0, index):
-        coefs = got[:, 0:R, :]
-        cen, rad = unpacked_shape(got[:, R : R + 8, :])
-        level = level0
-        while width > 1:
-            two = side_by_side(coefs)
-            path_pair[level, pl.ds(0, width // 2)] = two
-            path_co[level, pl.ds(0, width // 2)] = pair_coords(cen, rad, units)
-            coefs = lift(two)
-            cen, rad = merge_shapes(cen, rad)
-            width //= 2
-            level += 1
-        return coefs[0], packed_shape(cen[0], rad[0])
-
-    sub_levels, leaf_levels = ns.bit_length() - 1, nl.bit_length() - 1
-    for copy in sub_copies:
-        copy.wait()
-    top_coef, top_shape = climb(got_sub[...], ns, 0, sub_id)
-    root_b[0:R, :] = top_coef
-    root_b[R : R + 8, :] = top_shape
-    leaf_copies = [
-        send(root_b, got_leaf.at[leaf_id], leaf_send.at[o], leaf_recv.at[o], device)
-        for o, device in enumerate(leaf_devs)
-    ]
-    got_leaf[leaf_id] = root_b[...]
-
     dead = LD + 2 * REACH
     for ref in (c_all, v_all):
         ref[dead] = jnp.zeros(ref.shape[1:], BF16)
@@ -492,8 +466,36 @@
             product = dot_nt(*operands[s])
             lc[b * 4 + s] = jnp.where(lane_half, product[:R], product[R:])
 
+    def climb(got, width, level0, index):
+        coefs = got[:, 0:R, :]
+        cen, rad = unpacked_shape(got[:, R : R + 8, :])
+        level = level0
+        while width > 1:
+            two = side_by_side(coefs)
+            path_pair[level, pl.ds(0, width // 2)] = two
+            path_co[level, pl.ds(0, width // 2)] = pair_coords(cen, rad, units)
+            coefs = lift(two)
+            cen, rad = merge_shapes(cen, rad)
+            width //= 2
+            level += 1
+        return coefs[0], packed_shape(cen[0], rad[0])
+
+    sub_levels, leaf_levels = ns.bit_length() - 1, nl.bit_length() - 1
+    for copy in sub_copies:
+        copy.wait()
+    top_coef, top_shape = climb(got_sub[...], ns, 0, sub_id)
+    for b in range(2):
+        couple_four(b)
+    root_b[0:R, :] = top_coef
+    root_b[R : R + 8, :] = top_shape
+    leaf_copies = [
+        send(root_b, got_leaf.at[leaf_id], leaf_send.at[o], leaf_recv.at[o], device)
+        for o, device in enumerate(leaf_devs)
+    ]
+    got_leaf[leaf_id] = root_b[...]
+
     beside = 4
-    pl.loop(0, LD // 8 - beside)(couple_four)
+    pl.loop(2, LD // 8 - beside)(couple_four)
 
     for copy in leaf_copies:
         copy.wait()

time: 70.8 us -> 70.3 us (level)
  no operation moved by 1% of the time
where the time goes in v6:
time: 70.3 us; the launch traced here: 70.2 us
  Pallas kernels  67.1 us (95%)
  local copies, waits for them, and re-layouts  3.05 us (4%)
    pallas_call x1, Pallas kernels, per_device(): pl.pallas_call(body, out_shape=jax.ShapeDtypeStruct((R, LD * PT), F32), i...  67.1 us
    unnamed x1, local copies, waits for them, and re-layouts  3.05 us

profile of v6, /device:TPU:0, one launch (start us, length us, event | category | flops | bytes accessed | tf_op | source)
XLA Modules:
  0.0 70.2 jit_solution(2573605666877734518)
XLA Ops:
  0.0 67.1 %shard_map.64 = f32[32,16384]{1,0:T(8,128)} custom-call(bf16[32,16384]{1,0:T(8,128)(2,1)} %refs_0_.1, f32[3,16384]{1,0:T(4,128)} %refs_1_.1, bf16[128,64,128]{2,1,0:T(8,128)(2,1)} %refs_2_.1, f32[2,64,64]{2,1,0:T(8,128)} %refs_3_.1, s32[8,128]{1,0:T(8,128)} %bitcast.2, s32[8,128]{1,0:T(8,128)} %bitcast.3), custom_call_target="tpu_custom_call" | custom-call | flops 6000000000 | bytes 7000000 | tf_op jit(solution)/shard_map/pallas_call | solution.py:573
  67.1 3.0 %copy.8 = f32[32,16384]{1,0:T(8,128)} copy(f32[32,16384]{1,0:T(8,128)} %shard_map.64) | data formatting | bytes 4194304
